TPU v7x, 32 devices: a whole 2x2x4 slice. The times are simulated.
32 devices in a mesh: dp: 16 (over z, y, x), tensor: 2 (over core).
Axes of the slice: x: 2, y: 2, z: 4, core: 2. Of those that a mesh axis runs over, the one named last changes fastest.
Arguments:
- tokens: bfloat16 [6144, 576], P(('dp', 'tensor')), may hold values from -6 to 6
- w_attn: bfloat16 [2, 1536, 576], replicated, as said below
- attn_gain: float32 [2, 576], replicated, may hold values from 0.5 to 1.5
- w_gate: bfloat16 [2, 1536, 576], P(None, 'tensor'), may hold values from -0.25 to 0.25
- w_up: bfloat16 [2, 1536, 576], P(None, 'tensor'), may hold values from -0.25 to 0.25
- w_down: bfloat16 [2, 1536, 576], P(None, 'tensor'), may hold values from -0.15625 to 0.15625
- mlp_gain: float32 [2, 576], replicated, may hold values from 0.5 to 1.5
- seq_lengths: int32 [4], replicated, may hold values from 1024 to 2048, as said below
- cotangent: bfloat16 [6144, 576], P(('dp', 'tensor')), may hold values from -6 to 6
Outputs:
- out_act: float32 [6144, 576], P(('dp', 'tensor'))
- in_grad: float32 [6144, 576], P(('dp', 'tensor'))
- grad_attn: float32 [2, 1536, 576], P(None, ('dp', 'tensor'))
- grad_attn_gain: float32 [2, 576], replicated
- grad_gate: float32 [2, 1536, 576], P(None, ('tensor', 'dp'))
- grad_up: float32 [2, 1536, 576], P(None, ('tensor', 'dp'))
- grad_down: float32 [2, 1536, 576], P(None, ('tensor', 'dp'))
- grad_mlp_gain: float32 [2, 576], replicated
Inputs may be any that keep to these rules, and one draw needn't show every extreme that they name: `seq_lengths`: the lengths sum to 6144; one of them is exactly 2048. `w_attn`: independent entries of mean zero.
All inputs are finite; a program needn't handle non-finite values.
Results may differ from a plain program's by a relative error of at most 0.018.
Values may be sent and summed in bfloat16 or wider, within the bound.
A program may use at most 192 MiB of HBM per device.

v0:
```python
import jax
import jax.numpy as jnp
from jax import lax
from jax.sharding import PartitionSpec as P

H = 9
KV = 3
HD = 64
L_MAX = 2048


EPSILON = 1e-05
ROPE_BASE = 100000.0
MASKED = -1e30


def passed_along(array, axis, by):
    peers = lax.axis_size(axis)
    pairs = [(i, i + by) for i in range(peers) if 0 <= i + by < peers]
    return lax.ppermute(array, axis, pairs)


def sequence_start(places, starts):
    reached = starts[None, :] <= places[:, None]
    return jnp.max(jnp.where(reached, starts[None, :], -1), axis=1)


def rope_tables(relative):
    half_size = HD // 2
    frequencies = jnp.power(ROPE_BASE, -2.0 * jnp.arange(half_size, dtype=jnp.float32) / HD)
    angles = relative.astype(jnp.float32)[:, None] * frequencies[None, :]
    return (jnp.cos(angles)[:, None, :], jnp.sin(angles)[:, None, :])


def rotate(values, cosines, sines):
    half_size = values.shape[-1] // 2
    first_half = values[..., :half_size]
    second_half = values[..., half_size:]
    return jnp.concatenate(
        [first_half * cosines - second_half * sines, second_half * cosines + first_half * sines],
        axis=-1,
    )


def contract_rows(left, right):
    return lax.dot_general(
        left, right, (((1,), (1,)), ((), ())), preferred_element_type=jnp.float32
    )


def contract_cols(left, right):
    return lax.dot_general(
        left, right, (((0,), (0,)), ((), ())), preferred_element_type=jnp.float32
    )


def rms_parts(values):
    inverse = lax.rsqrt(jnp.mean(values * values, axis=-1, keepdims=True) + EPSILON)
    return (values * inverse, inverse)


def norm_back(grad_out, ratio, inverse, gain_vec):
    scaled = grad_out * gain_vec
    input_grad = inverse * (scaled - ratio * jnp.mean(scaled * ratio, axis=-1, keepdims=True))
    return (input_grad, jnp.sum(grad_out * ratio, axis=0))


def fetch_window(own_rows, reach_back, own_count):

    def pass_on(running, unused):
        moved_rows = passed_along(running, ("dp", "tensor"), 1)
        return (moved_rows, moved_rows)

    _, arrivals = lax.scan(pass_on, own_rows, None, length=reach_back)
    older_rows = arrivals[::-1].reshape(reach_back * own_count, own_rows.shape[1])
    return jnp.concatenate([older_rows, own_rows], axis=0)


def return_window(gradients, reach_back, own_count):
    row_width = gradients.shape[1]
    pieces = gradients.reshape(reach_back + 1, own_count, row_width)

    def pass_back(running, local_piece):
        moved_rows = passed_along(running.astype(jnp.bfloat16), ("dp", "tensor"), -1).astype(
            running.dtype
        )
        return (moved_rows + local_piece, None)

    summed, _ = lax.scan(pass_back, pieces[0], pieces[1:])
    return summed


def piece_rows_for(total_rows, own_count):
    shard_count = total_rows // own_count
    for divisions in range(1, shard_count + 1):
        return total_rows // divisions
    return own_count


def masked_scores(grouped, key_block, offset, piece_rows, query_places, query_starts, starts):
    key_places = offset + jnp.arange(piece_rows, dtype=jnp.int32)
    key_starts = sequence_start(key_places, starts)
    allowed = (key_starts[None, :] == query_starts[:, None]) & (
        key_places[None, :] <= query_places[:, None]
    )
    scores = 0.125 * jnp.einsum(
        "tkgd,skd->kgts", grouped, key_block[:, 0], preferred_element_type=jnp.float32
    )
    return (jnp.where(allowed[None, None], scores, MASKED), allowed)


def attend_forward(queries, window, query_places, query_starts, first_key, starts, piece_rows):
    own_count = queries.shape[0]
    groups = H // KV
    grouped = queries.reshape(own_count, KV, groups, HD)
    key_sets = window.reshape(window.shape[0] // piece_rows, piece_rows, 2, KV, HD)
    offsets = first_key + piece_rows * jnp.arange(key_sets.shape[0], dtype=jnp.int32)

    def first_pass(running, scan_item):
        highest, summed = running
        key_block, offset = scan_item
        scores, allowed = masked_scores(
            grouped, key_block, offset, piece_rows, query_places, query_starts, starts
        )
        newest = jnp.maximum(highest, jnp.max(scores, axis=-1))
        exp_terms = jnp.where(allowed[None, None], jnp.exp(scores - newest[..., None]), 0.0)
        summed = summed * jnp.exp(highest - newest) + jnp.sum(exp_terms, axis=-1)
        return ((newest, summed), None)

    stat_shape = (KV, groups, own_count)
    start_state = (jnp.full(stat_shape, MASKED, jnp.float32), jnp.zeros(stat_shape, jnp.float32))
    (highest, summed), _ = lax.scan(first_pass, start_state, (key_sets, offsets))
    logsum = highest + jnp.log(summed)

    def second_pass(accumulated, scan_item):
        key_block, offset = scan_item
        scores, allowed = masked_scores(
            grouped, key_block, offset, piece_rows, query_places, query_starts, starts
        )
        weights = jnp.where(allowed[None, None], jnp.exp(scores - logsum[..., None]), 0.0).astype(
            jnp.bfloat16
        )
        product = jnp.einsum(
            "kgts,skd->tkgd", weights, key_block[:, 1], preferred_element_type=jnp.float32
        )
        return (accumulated + product, None)

    accumulated, _ = lax.scan(
        second_pass, jnp.zeros((own_count, KV, groups, HD), jnp.float32), (key_sets, offsets)
    )
    return (accumulated.reshape(own_count, H * HD), logsum)


def attend_backward(
    queries, window, grad_mixed, logsum, query_places, query_starts, first_key, starts, piece_rows
):
    own_count = queries.shape[0]
    groups = H // KV
    grouped = queries.reshape(own_count, KV, groups, HD)
    grad_grouped = grad_mixed.reshape(own_count, KV, groups, HD)
    key_sets = window.reshape(window.shape[0] // piece_rows, piece_rows, 2, KV, HD)
    offsets = first_key + piece_rows * jnp.arange(key_sets.shape[0], dtype=jnp.int32)

    def chances(key_block, offset):
        scores, allowed = masked_scores(
            grouped, key_block, offset, piece_rows, query_places, query_starts, starts
        )
        weights = jnp.where(allowed[None, None], jnp.exp(scores - logsum[..., None]), 0.0)
        slopes = jnp.einsum(
            "tkgd,skd->kgts", grad_grouped, key_block[:, 1], preferred_element_type=jnp.float32
        )
        return (weights, slopes)

    def delta_pass(running, scan_item):
        weights, slopes = chances(scan_item[0], scan_item[1])
        return (running + jnp.sum(weights * slopes, axis=-1), None)

    row_delta, _ = lax.scan(
        delta_pass, jnp.zeros((KV, groups, own_count), jnp.float32), (key_sets, offsets)
    )

    def grad_pass(running, scan_item):
        key_block, offset = scan_item
        weights, slopes = chances(key_block, offset)
        score_grads = (weights * (slopes - row_delta[..., None])).astype(jnp.bfloat16)
        running = running + jnp.einsum(
            "kgts,skd->tkgd", score_grads, key_block[:, 0], preferred_element_type=jnp.float32
        )
        key_grads = 0.125 * jnp.einsum(
            "kgts,tkgd->skd", score_grads, grouped, preferred_element_type=jnp.float32
        )
        value_grads = jnp.einsum(
            "kgts,tkgd->skd",
            weights.astype(jnp.bfloat16),
            grad_grouped,
            preferred_element_type=jnp.float32,
        )
        return (running, jnp.stack([key_grads, value_grads], axis=1))

    query_grads, pieces = lax.scan(
        grad_pass, jnp.zeros((own_count, KV, groups, HD), jnp.float32), (key_sets, offsets)
    )
    return (
        0.125 * query_grads.reshape(own_count, H, HD),
        pieces.reshape(window.shape[0], 2 * KV * HD),
    )


def reduce_grads(attn_part, gate_part, up_part, down_part, gain_a_part, gain_m_part):
    attn_sum = lax.psum_scatter(attn_part, ("dp", "tensor"), scatter_dimension=1, tiled=True)
    gate_sum, up_sum, down_sum = (
        lax.psum_scatter(gate_part, "dp", scatter_dimension=1, tiled=True),
        lax.psum_scatter(up_part, "dp", scatter_dimension=1, tiled=True),
        lax.psum_scatter(down_part, "dp", scatter_dimension=1, tiled=True),
    )
    gain_a_sum, gain_m_sum = lax.psum((gain_a_part, gain_m_part), ("dp", "tensor"))
    return (attn_sum, gate_sum, up_sum, down_sum, gain_a_sum, gain_m_sum)


def body(tokens, w_attn, attn_gain, w_gate, w_up, w_down, mlp_gain, seq_lengths, cotangent):
    own_count = tokens.shape[0]
    layer_count = w_attn.shape[0]
    qkv_rows = (H + 2 * KV) * HD
    reach_back = (L_MAX + own_count - 2) // own_count
    window_rows = (reach_back + 1) * own_count
    piece_rows = piece_rows_for(window_rows, own_count)
    seq_ends = jnp.cumsum(seq_lengths)
    starts = seq_ends - seq_lengths
    first_place = lax.axis_index(("dp", "tensor")) * own_count
    query_places = first_place + jnp.arange(own_count, dtype=jnp.int32)
    query_starts = sequence_start(query_places, starts)
    first_key = first_place - reach_back * own_count
    cosines, sines = rope_tables(query_places - query_starts)
    stream = tokens.astype(jnp.float32)
    stored = []
    for layer_index in range(layer_count):
        attn_w = w_attn[layer_index]
        ratio_a, inverse_a = rms_parts(stream)
        normed = (ratio_a * attn_gain[layer_index]).astype(jnp.bfloat16)
        projected = contract_rows(normed, attn_w[:qkv_rows])
        q_lin = projected[:, : H * HD].reshape(own_count, H, HD)
        k_lin = projected[:, H * HD : (H + KV) * HD].reshape(own_count, KV, HD)
        queries = rotate(q_lin, cosines, sines).astype(jnp.bfloat16)
        key_rows = rotate(k_lin, cosines, sines).astype(jnp.bfloat16).reshape(own_count, KV * HD)
        kv_own = jnp.concatenate(
            [key_rows, projected[:, (H + KV) * HD :].astype(jnp.bfloat16)], axis=1
        )
        window = fetch_window(kv_own, reach_back, own_count)
        mixed_float, logsum = attend_forward(
            queries, window, query_places, query_starts, first_key, starts, piece_rows
        )
        mixed_heads = mixed_float.astype(jnp.bfloat16)
        middle = stream + contract_rows(mixed_heads, attn_w[qkv_rows:])
        ratio_m, inverse_m = rms_parts(middle)
        normed_m = (ratio_m * mlp_gain[layer_index]).astype(jnp.bfloat16)
        gathered = lax.all_gather(normed_m, "tensor", axis=0, tiled=True)
        gate_pre = contract_rows(gathered, w_gate[layer_index])
        up_pre = contract_rows(gathered, w_up[layer_index])
        hidden = (jax.nn.silu(gate_pre) * up_pre).astype(jnp.bfloat16)
        down_w = w_down[layer_index]
        stored.append(
            (
                ratio_a,
                inverse_a,
                normed,
                queries,
                window,
                mixed_heads,
                logsum,
                ratio_m,
                inverse_m,
                gathered,
                gate_pre,
                up_pre,
                hidden,
            )
        )
        stream = middle + lax.psum_scatter(
            jnp.dot(hidden, down_w, preferred_element_type=jnp.float32).astype(jnp.bfloat16),
            "tensor",
            scatter_dimension=0,
            tiled=True,
        ).astype(jnp.float32)
    upstream = cotangent.astype(jnp.float32)
    raw_parts = []
    for layer_index in reversed(range(layer_count)):
        (
            ratio_a,
            inverse_a,
            normed,
            queries,
            window,
            mixed_heads,
            logsum,
            ratio_m,
            inverse_m,
            gathered,
            gate_pre,
            up_pre,
            hidden,
        ) = stored[layer_index]
        attn_w = w_attn[layer_index]
        gate_w = w_gate[layer_index]
        up_w = w_up[layer_index]
        down_w = w_down[layer_index]
        down_all = lax.all_gather(upstream.astype(jnp.bfloat16), "tensor", axis=0, tiled=True)
        grad_down = contract_cols(hidden, down_all)
        grad_hidden = contract_rows(down_all, down_w)
        gate_sigmoid = jax.nn.sigmoid(gate_pre)
        grad_gate_pre = (
            grad_hidden * up_pre * gate_sigmoid * (1.0 + gate_pre * (1.0 - gate_sigmoid))
        ).astype(jnp.bfloat16)
        grad_up_pre = (grad_hidden * gate_pre * gate_sigmoid).astype(jnp.bfloat16)
        grad_gate = contract_cols(grad_gate_pre, gathered)
        grad_up = contract_cols(grad_up_pre, gathered)
        grad_normed_m = lax.psum_scatter(
            (
                jnp.dot(grad_gate_pre, gate_w, preferred_element_type=jnp.float32)
                + jnp.dot(grad_up_pre, up_w, preferred_element_type=jnp.float32)
            ).astype(jnp.bfloat16),
            "tensor",
            scatter_dimension=0,
            tiled=True,
        ).astype(jnp.float32)
        back_m, gain_m_grad = norm_back(grad_normed_m, ratio_m, inverse_m, mlp_gain[layer_index])
        grad_middle = upstream + back_m
        branch_in = grad_middle.astype(jnp.bfloat16)
        grad_out_proj = contract_cols(branch_in, mixed_heads)
        grad_mixed = jnp.dot(
            branch_in, attn_w[qkv_rows:], preferred_element_type=jnp.float32
        ).astype(jnp.bfloat16)
        query_grads, window_grads = attend_backward(
            queries,
            window,
            grad_mixed,
            logsum,
            query_places,
            query_starts,
            first_key,
            starts,
            piece_rows,
        )
        own_grads = return_window(window_grads, reach_back, own_count)
        key_back = rotate(
            own_grads[:, : KV * HD].reshape(own_count, KV, HD), cosines, -sines
        ).reshape(own_count, KV * HD)
        query_back = rotate(query_grads, cosines, -sines).reshape(own_count, H * HD)
        grad_projected = jnp.concatenate(
            [query_back, key_back, own_grads[:, KV * HD :]], axis=1
        ).astype(jnp.bfloat16)
        grad_qkv = contract_cols(grad_projected, normed)
        grad_normed = jnp.dot(grad_projected, attn_w[:qkv_rows], preferred_element_type=jnp.float32)
        back_a, gain_a_grad = norm_back(grad_normed, ratio_a, inverse_a, attn_gain[layer_index])
        upstream = grad_middle + back_a
        attn_grad = jnp.concatenate([grad_qkv, grad_out_proj], axis=0)
        raw_parts.append((attn_grad, grad_gate, grad_up, grad_down, gain_a_grad, gain_m_grad))
    ordered = raw_parts[::-1]
    stacked = tuple(
        (
            jnp.stack([layer_entry[slot_index] for layer_entry in ordered], axis=0)
            for slot_index in range(6)
        )
    )
    results = reduce_grads(stacked[0], stacked[1], stacked[2], stacked[3], stacked[4], stacked[5])
    attn_sum, gate_sum, up_sum, down_sum, gain_a_sum, gain_m_sum = results
    return (stream, upstream, attn_sum, gain_a_sum, gate_sum, up_sum, down_sum, gain_m_sum)


def solution(mesh):
    placed = (
        P(("dp", "tensor"), None),
        P(),
        P(),
        P(None, "tensor", None),
        P(None, "tensor", None),
        P(None, "tensor", None),
        P(),
        P(),
        P(("dp", "tensor"), None),
    )
    return jax.shard_map(
        body,
        mesh=mesh,
        in_specs=placed,
        out_specs=(
            P(("dp", "tensor"), None),
            P(("dp", "tensor"), None),
            P(None, ("dp", "tensor"), None),
            P(),
            P(None, ("tensor", "dp"), None),
            P(None, ("tensor", "dp"), None),
            P(None, ("tensor", "dp"), None),
            P(),
        ),
        check_vma=False,
    )
```

profile of v0, /device:TPU:0, one launch (start us, length us, event | category | flops | bytes accessed | tf_op | source)
XLA Modules:
  0.0 1240.3 jit_solution(16461252322489303561)
XLA Ops:
  14.4 70.8 %while.8 = (s32[]{:T(128)}, bf16[192,384]{1,0:T(8,128)(2,1)S(1)}, bf16[11,192,384]{2,1,0:T(8,128)(2,1)S(1)}, s32[]{:T(128)}) while((s32[]{:T(128)}, bf16[192,384]{1,0:T(8,128)(2,1)S(1)}, bf16[11,192,384]{2,1,0:T(8,128)(2,1)S(1)}, s32[]{:T(128)}) %tuple.125), condition=%wide.region_4.5_spmd, body=%wide.region_3.4_spmd.sunk | while | flops 2 | bytes 1179753 | solution.py:74
  70.3 6.4 collective-permute-start
  77.7 6.4 collective-permute-start
  96.8 7.5 fusion.6
  104.3 10.2 select_reduce_fusion.1
  114.6 8.7 convolution_convert_fusion.3
  138.6 23.3 %reduce-scatter.5.cloned.1.call-done = bf16[192,576]{1,0:T(8,128)(2,1)} async-done(((bf16[384,576]{1,0:T(8,128)(2,1)}), bf16[192,576]{1,0:T(8,128)(2,1)}) %reduce-scatter.5.cloned.1.call-update) | async-done | bytes 221200 | tf_op jit(solution)/shard_map/reduce_scatter | solution.py:278
  167.7 76.3 %while.9 = (s32[]{:T(128)}, bf16[192,384]{1,0:T(8,128)(2,1)S(1)}, bf16[11,192,384]{2,1,0:T(8,128)(2,1)}, s32[]{:T(128)}) while((s32[]{:T(128)}, bf16[192,384]{1,0:T(8,128)(2,1)S(1)}, bf16[11,192,384]{2,1,0:T(8,128)(2,1)}, s32[]{:T(128)}) %tuple.128), condition=%wide.region_12.13_spmd, body=%wide.region_11.12_spmd.sunk | while | flops 2 | bytes 1179753 | solution.py:74
  227.8 6.4 collective-permute-start.1
  235.9 6.4 collective-permute-start.1
  257.2 7.5 fusion.7
  264.7 10.2 select_reduce_fusion
  275.0 8.5 convolution_convert_fusion.2
  285.7 17.8 %all_gather.13 = bf16[384,576]{1,0:T(8,128)(2,1)S(1)} all-gather(bf16[192,576]{1,0:T(8,128)(2,1)S(1)} %multiply_convert_fusion.6), channel_id=1, replica_groups=mesh['dp'=16,'tensor'=2] {'tensor'}, dimensions={0}, use_global_device_ids=true | all-gather | bytes 663552 | tf_op jit(solution)/shard_map/all_gather | solution.py:256
  312.0 22.5 %reduce-scatter.9.cloned.1.call-done = bf16[192,576]{1,0:T(8,128)(2,1)} async-done(((bf16[384,576]{1,0:T(8,128)(2,1)}), bf16[192,576]{1,0:T(8,128)(2,1)}) %reduce-scatter.9.cloned.1.call-update) | async-done | bytes 221200 | tf_op jit(solution)/shard_map/reduce_scatter | solution.py:316
  336.4 10.1 reduce-scatter.7.cloned.1.call-done
  351.8 14.3 %fusion.3 = (f32[3,3,192]{2,1,0:T(4,128)S(1)}, f32[3,2304,192,3]{1,2,3,0:T(8,128)}) fusion(f32[3,3,192]{2,1,0:T(4,128)S(1)} %log_add_fusion, f32[3,2304,192,3]{1,2,3,0:T(8,128)} %get-tuple-element.468, pred[192,2304]{1,0:T(8,128)(4,1)S(1)} %compare_and_fusion, bf16[192,3,3,64]{0,3,2,1:T(8,128)(2,1)} %bitcast.350, bf16[2112,2,3,64]{0,3,2,1:T(8,128)(2,1)} %copy-done.3, ...), kind=kOutput, calls=%fused_computation.11 | convolution fusion | flops 535263552 | bytes 34297344 | tf_op jit(solution)/shard_map/while/body/eval_jaxpr/tkgd,skd->kgts/dot_general | solution.py:169
  367.8 8.3 fusion.5
  390.5 6.3 slice.256
  402.9 82.8 %while.10 = (s32[]{:T(128)}, f32[192,384]{1,0:T(8,128)S(1)}, f32[11,192,384]{2,1,0:T(8,128)}, s32[]{:T(128)}) while((s32[]{:T(128)}, f32[192,384]{1,0:T(8,128)S(1)}, f32[11,192,384]{2,1,0:T(8,128)}, s32[]{:T(128)}) %tuple.131), condition=%wide.region_21.22_spmd, body=%wide.region_20.21_spmd.sunk | while | flops 221186 | bytes 1769577 | solution.py:89
  491.9 6.4 all_gather.15
  505.8 20.1 %reduce-scatter.11.cloned.1.call-done = bf16[192,576]{1,0:T(8,128)(2,1)} async-done(((bf16[384,576]{1,0:T(8,128)(2,1)}), bf16[192,576]{1,0:T(8,128)(2,1)}) %reduce-scatter.11.cloned.1.call-update) | async-done | bytes 221200 | tf_op jit(solution)/shard_map/reduce_scatter | solution.py:316
  531.5 15.1 %fusion = (f32[3,3,192]{2,1,0:T(4,128)S(1)}, f32[3,2304,192,3]{1,2,3,0:T(8,128)}) fusion(f32[3,3,192]{2,1,0:T(4,128)S(1)} %copy-done.65, f32[3,2304,192,3]{1,2,3,0:T(8,128)} %get-tuple-element.462, pred[192,2304]{1,0:T(8,128)(4,1)S(1)} %compare_and_fusion, bf16[192,3,3,64]{0,3,2,1:T(8,128)(2,1)} %bitcast.348, bf16[2112,2,3,64]{0,3,2,1:T(8,128)(2,1)} %copy-done.2, ...), kind=kOutput, calls=%fused_computation.6 | convolution fusion | flops 535263552 | bytes 34297344 | tf_op jit(solution)/shard_map/while/body/eval_jaxpr/tkgd,skd->kgts/dot_general | solution.py:169
  547.6 8.3 fusion.2
  582.7 82.7 %while.11 = (s32[]{:T(128)}, f32[192,384]{1,0:T(8,128)S(1)}, f32[11,192,384]{2,1,0:T(8,128)}, s32[]{:T(128)}) while((s32[]{:T(128)}, f32[192,384]{1,0:T(8,128)S(1)}, f32[11,192,384]{2,1,0:T(8,128)}, s32[]{:T(128)}) %tuple.134), condition=%wide.region_27.28_spmd, body=%wide.region_26.27_spmd.sunk | while | flops 221186 | bytes 1769577 | solution.py:89
  676.6 12.4 %copy.141 = f32[2,1536,576]{2,0,1:T(2,128)} copy(f32[2,1536,576]{1,2,0:T(8,128)} %pad_maximum_fusion) | data formatting | bytes 14155776 | tf_op jit(solution)/shard_map/stack | solution.py:360
  697.8 7.6 copy.144
  709.0 7.6 copy.143
  720.1 7.5 copy.142
  731.6 59.3 %all-reduce.4 = (f32[2,576]{1,0:T(2,128)}, f32[2,576]{1,0:T(2,128)}) all-reduce(f32[2,576]{1,0:T(2,128)S(1)} %get-tuple-element.477, f32[2,576]{1,0:T(2,128)S(1)} %get-tuple-element.478), channel_id=1, replica_groups=mesh['dp'=16,'tensor'=2] {'dp','tensor'}, use_global_device_ids=true, to_apply=%region_32.33 | all-reduce | flops 2304 | bytes 18432 | tf_op jit(solution)/shard_map/psum | solution.py:216
  791.9 90.0 %all-reduce.9.cloned.1.call-done = f32[2,1536,576]{2,0,1:T(2,128)} async-done(((f32[2,1536,576]{2,0,1:T(2,128)}), f32[2,1536,576]{2,0,1:T(2,128)}) %all-reduce.9.cloned.1.call-update) | async-done | bytes 7077904
  883.7 345.4 %all-reduce.11.cloned.1.call-done = (f32[2,768,576]{2,0,1:T(2,128)}, f32[2,768,576]{2,0,1:T(2,128)}, f32[2,768,576]{2,0,1:T(2,128)}) async-done(((f32[2,768,576]{2,0,1:T(2,128)}, f32[2,768,576]{2,0,1:T(2,128)}, f32[2,768,576]{2,0,1:T(2,128)}), (f32[2,768,576]{2,0,1:T(2,128)}, f32[2,768,576]{2,0,1:T(2,128)}, f32[2,768,576]{2,0,1:T(2,128)})) %all-reduce.11.cloned.1.call-update) | async-done | bytes 10616848
  (521 shorter events, 462.1 us)
Async XLA Ops:
  7.2 154.8 %reduce-scatter.5.cloned.1.call-start = ((), (), s32[]{:S(2)}) async-start(), calls=%async_computation.4 | async-start | bytes 737280 | tf_op jit(solution)/shard_map/reduce_scatter | solution.py:278
  17.8 6.6 collective-permute-start
  24.5 6.5 collective-permute-start
  31.0 6.5 collective-permute-start
  37.6 6.5 collective-permute-start
  44.1 6.5 collective-permute-start
  50.6 6.5 collective-permute-start
  57.2 6.5 collective-permute-start
  63.7 6.5 collective-permute-start
  70.3 7.4 collective-permute-start
  77.7 7.4 collective-permute-start
  136.3 198.3 %reduce-scatter.9.cloned.1.call-start = ((), (), s32[]{:S(2)}) async-start(), calls=%async_computation.6 | async-start | bytes 737280 | tf_op jit(solution)/shard_map/reduce_scatter | solution.py:316
  220.6 6.5 collective-permute-start.1
  227.8 7.3 collective-permute-start.1
  235.9 7.3 collective-permute-start.1
  309.1 37.4 %reduce-scatter.7.cloned.1.call-start = ((), (), s32[]{:S(2)}) async-start(), calls=%async_computation.5 | async-start | bytes 737280 | tf_op jit(solution)/shard_map/reduce_scatter | solution.py:278
  312.0 214.0 %reduce-scatter.11.cloned.1.call-start = ((), (), s32[]{:S(2)}) async-start(), calls=%async_computation.7 | async-start | bytes 737280 | tf_op jit(solution)/shard_map/reduce_scatter | solution.py:316
  414.6 6.5 collective-permute-start.2
  437.0 6.5 collective-permute-start.2
  444.5 6.6 collective-permute-start.2
  452.2 7.4 collective-permute-start.2
  460.6 7.4 collective-permute-start.2
  469.0 7.4 collective-permute-start.2
  477.4 7.4 collective-permute-start.2
  502.3 379.7 %all-reduce.9.cloned.1.call-start = ((), (), s32[]{:S(2)}) async-start(), calls=%async_computation.8 | async-start | bytes 15728640
  594.2 6.5 collective-permute-start.3
  624.2 6.6 collective-permute-start.3
  631.8 7.4 collective-permute-start.3
  640.2 7.4 collective-permute-start.3
  648.6 7.4 collective-permute-start.3
  657.0 7.4 collective-permute-start.3
  689.1 540.0 %all-reduce.11.cloned.1.call-start = ((), (), s32[]{:S(2)}) async-start(), calls=%async_computation.9 | async-start | bytes 23592960
  (113 other events, 1445.4 us)
Sparse Core Ops, SparseCore 0:
  136.4 25.5 reduce-scatter.4
  309.2 25.2 reduce-scatter.8
  337.4 9.0 reduce-scatter.6
  502.4 23.4 reduce-scatter.10
  689.2 192.7 all-reduce.8
  888.3 340.7 all-reduce.10
where the time goes:
time: 1250 us; the launch traced here: 1240 us
  waiting for transfers between devices  647 us (52%)
  starting transfers between devices  146 us (12%)
  matrix products  126 us (10%)
  local copies, waits for them, and re-layouts  116 us (9%)
  other arithmetic  95.2 us (8%)
  blocking collectives  92 us (7%)
  between operations  16.5 us (1%)
    unnamed x8, waiting for transfers between devices  436 us
    ppermute x44, starting transfers between devices, passed_along(): return lax.ppermute(array, axis, pairs)  145 us
    ppermute x44, waiting for transfers between devices, passed_along(): return lax.ppermute(array, axis, pairs)  136 us
    psum x1, blocking collectives, reduce_grads(): lax.psum((gain_a_part, gain_m_part), ('dp', 'tensor'))  59.3 us
    reduce_scatter x2, waiting for transfers between devices, body(): lax.psum_scatter((jnp.dot(grad_gate_pre, gate_w, preferred_element_type=j...  42.6 us
    another operation x8, local copies, waits for them, and re-layouts, body(): jnp.stack([layer_entry[slot_index] for layer_entry in ordered], axis=0)  35.1 us
    reduce_scatter x2, waiting for transfers between devices, body(): lax.psum_scatter(jnp.dot(hidden, down_w, preferred_element_type=jnp.float...  33.4 us
    dot_general x2, matrix products, chances(): jnp.einsum('tkgd,skd->kgts', grad_grouped, key_block[:, 1], preferred_ele...  29.4 us
  transfers between devices with their start and end apart: 50, of which 50 were waited for; matrix products, arithmetic and copies ran while one was open for 4% of the time, Pallas kernels for 0%

commit v1 on v0

v1 whole, which is shorter than its diff:
```python
import functools

import jax
import jax.numpy as jnp
from jax import lax
from jax.experimental import pallas as pl
from jax.experimental.pallas import tpu as pltpu
from jax.sharding import PartitionSpec as P

H = 9
KV = 3
GROUPS = H // KV
HD = 64
TILE = 2 * HD
L_MAX = 2048

EPSILON = 1e-05
ROPE_BASE = 100000.0
MASKED = -1e30
MESH = pl.DeviceIdType.MESH
AXES = ("dp", "tensor")
VMEM_LIMIT = 56 * 1024 * 1024


def rows_by_rows(left, right):
    return lax.dot_general(
        left, right, (((1,), (1,)), ((), ())), preferred_element_type=jnp.float32
    )


def cols_by_cols(left, right):
    return lax.dot_general(
        left, right, (((0,), (0,)), ((), ())), preferred_element_type=jnp.float32
    )


def plain_dot(left, right):
    return jnp.dot(left, right, preferred_element_type=jnp.float32)


def sequence_start(places, starts):
    reached = starts[None, :] <= places[:, None]
    return jnp.max(jnp.where(reached, starts[None, :], -1), axis=1)


def rms_parts(values):
    inverse = lax.rsqrt(jnp.mean(values * values, axis=-1, keepdims=True) + EPSILON)
    return (values * inverse, inverse)


def norm_back(grad_out, ratio, inverse, gain_vec):
    scaled = grad_out * gain_vec
    input_grad = inverse * (scaled - ratio * jnp.mean(scaled * ratio, axis=-1, keepdims=True))
    return (input_grad, jnp.sum(grad_out * ratio, axis=0, keepdims=True))


def swap_halves(values):
    lane = lax.broadcasted_iota(jnp.int32, values.shape, 1)
    return jnp.where(
        lane < HD // 2,
        pltpu.roll(values, TILE - HD // 2, 1),
        pltpu.roll(values, HD // 2, 1),
    )


def call(kernel, out_shape, scratch=(), **params):
    return pl.pallas_call(
        kernel,
        out_shape=out_shape,
        scratch_shapes=list(scratch),
        compiler_params=pltpu.CompilerParams(vmem_limit_bytes=VMEM_LIMIT, **params),
    )


def project_kernel(x_ref, gain_ref, w_ref, cq_ref, ckv_ref, sn_ref, q_ref, kv_ref, a_ref):
    own = x_ref.shape[0]
    ratio, _ = rms_parts(x_ref[...])
    normed = (ratio * gain_ref[...]).astype(jnp.bfloat16)
    a_ref[...] = normed
    sines = sn_ref[...]
    for head in range(H + KV):
        lin = rows_by_rows(normed, w_ref[head * TILE : (head + 1) * TILE, :])
        cosines = cq_ref[...] if head < H else ckv_ref[...]
        turned = (lin * cosines + swap_halves(lin) * sines).astype(jnp.bfloat16)
        if head < H:
            rows = slice((head % GROUPS) * own, (head % GROUPS + 1) * own)
            q_ref[head // GROUPS, rows, :] = turned * jnp.bfloat16(0.125)
        else:
            kv_ref[:, (head - H) * TILE : (head - H + 1) * TILE] = turned


def mesh_id(index, pair):
    return {"dp": lax.div(index, pair), "tensor": lax.rem(index, pair)}


def greet(me, count, reach, step):
    barrier = pltpu.get_barrier_semaphore()
    pair = lax.axis_size("tensor")
    for by in range(1, reach + 1):
        sender = me + step * by

        @pl.when((sender >= 0) & (sender < count))
        def _():
            pl.semaphore_signal(
                barrier, inc=1, device_id=mesh_id(sender, pair), device_id_type=MESH
            )

    copied_to = jnp.minimum(count - 1 - me if step < 0 else me, reach)

    @pl.when(copied_to > 0)
    def _():
        pl.semaphore_wait(barrier, copied_to)


def fetch_kernel(count, reach, own_ref, window_ref, send_sem, recv_sem):
    pair = lax.axis_size("tensor")
    me = lax.axis_index("dp") * pair + lax.axis_index("tensor")
    greet(me, count, reach, -1)

    def send(by):
        return pltpu.make_async_remote_copy(
            src_ref=own_ref,
            dst_ref=window_ref.at[reach - by],
            send_sem=send_sem.at[by - 1],
            recv_sem=recv_sem.at[by - 1],
            device_id=mesh_id(me + by, pair),
            device_id_type=MESH,
        )

    for by in range(1, reach + 1):

        @pl.when(me + by < count)
        def _():
            send(by).start()

    window_ref[reach] = own_ref[...]
    for by in range(1, reach + 1):

        @pl.when(me - by < 0)
        def _():
            window_ref[reach - by] = jnp.zeros(own_ref.shape, own_ref.dtype)

    for by in range(1, reach + 1):

        @pl.when(me - by >= 0)
        def _():
            send(by).wait_recv()

        @pl.when(me + by < count)
        def _():
            send(by).wait_send()


def return_kernel(count, reach, grads_ref, sum_ref, held, send_sem, recv_sem):
    pair = lax.axis_size("tensor")
    me = lax.axis_index("dp") * pair + lax.axis_index("tensor")
    greet(me, count, reach, 1)

    def send(by):
        return pltpu.make_async_remote_copy(
            src_ref=grads_ref.at[reach - by],
            dst_ref=held.at[by - 1],
            send_sem=send_sem.at[by - 1],
            recv_sem=recv_sem.at[by - 1],
            device_id=mesh_id(me - by, pair),
            device_id_type=MESH,
        )

    for by in range(reach, 0, -1):

        @pl.when(me - by >= 0)
        def _():
            send(by).start()

    sum_ref[...] = grads_ref[reach].astype(jnp.float32)
    for by in range(1, reach + 1):

        @pl.when(me + by < count)
        def _():
            send(by).wait_recv()
            sum_ref[...] += held[by - 1].astype(jnp.float32)

        @pl.when(me - by >= 0)
        def _():
            send(by).wait_send()


def allowed_pairs(chunk, rows, low_ref, high_ref):
    place = chunk * rows + lax.broadcasted_iota(jnp.int32, (rows, low_ref.shape[1]), 0)
    return (place >= low_ref[...]) & (place <= high_ref[...])


def attend_kernel(
    chunk_rows,
    q_ref,
    win_ref,
    low_ref,
    high_ref,
    x_ref,
    wo_ref,
    gain_ref,
    wg_ref,
    wu_ref,
    wd_ref,
    x_out_ref,
    mid_ref,
    m_ref,
    gate_ref,
    up_ref,
    hidden_ref,
    o_ref,
    lse_ref,
    acc_ref,
    top_ref,
    total_ref,
):
    own = x_ref.shape[0]
    chunks = win_ref.shape[0] // chunk_rows
    acc_ref[...] = jnp.zeros_like(acc_ref)
    total_ref[...] = jnp.zeros_like(total_ref)
    top_ref[...] = jnp.full_like(top_ref, MASKED)

    def step(chunk, unused):
        allowed = allowed_pairs(chunk, chunk_rows, low_ref, high_ref)
        start = pl.multiple_of(chunk * chunk_rows, chunk_rows)
        for j in range(KV):
            tile = win_ref[pl.ds(start, chunk_rows), j * TILE : (j + 1) * TILE]
            scores = jnp.where(allowed, rows_by_rows(tile, q_ref[j]), MASKED)
            highest = top_ref[j]
            newest = jnp.maximum(highest, jnp.max(scores, axis=0, keepdims=True))
            terms = jnp.exp(scores - newest)
            decay = jnp.exp(highest - newest)
            top_ref[j] = newest
            total_ref[j] = total_ref[j] * decay + jnp.sum(terms, axis=0, keepdims=True)
            acc_ref[j] = acc_ref[j] * decay + cols_by_cols(tile, terms.astype(jnp.bfloat16))
        return unused

    lax.fori_loop(0, chunks, step, 0)
    middle = x_ref[...]
    for j in range(KV):
        lse_ref[j] = top_ref[j] + jnp.log(total_ref[j])
        mixed = (acc_ref[j] / total_ref[j]).T
        o_ref[j] = mixed
        low = mixed.astype(jnp.bfloat16)
        for g in range(GROUPS):
            middle = middle + plain_dot(low[g * own : (g + 1) * own], wo_ref[j * GROUPS + g])
    mid_ref[...] = middle
    ratio, _ = rms_parts(middle)
    normed = (ratio * gain_ref[...]).astype(jnp.bfloat16)
    m_ref[...] = normed
    gate = rows_by_rows(normed, wg_ref[...])
    up = rows_by_rows(normed, wu_ref[...])
    gate_ref[...] = gate
    up_ref[...] = up
    hidden = (gate * jax.nn.sigmoid(gate) * up).astype(jnp.bfloat16)
    hidden_ref[...] = hidden
    x_out_ref[...] = middle + plain_dot(hidden, wd_ref[...])


def mlp_back_kernel(
    gx_ref,
    mid_ref,
    gate_ref,
    up_ref,
    gain_ref,
    wg_ref,
    wu_ref,
    wd_ref,
    gy_ref,
    ggate_ref,
    gup_ref,
    gmid_ref,
    go_ref,
    ggain_ref,
):
    gx = gx_ref[...].astype(jnp.float32)
    gy = gx.astype(jnp.bfloat16)
    gy_ref[...] = gy
    gh = rows_by_rows(gy, wd_ref[...])
    gate = gate_ref[...]
    sig = jax.nn.sigmoid(gate)
    ggate = (gh * up_ref[...] * sig * (1.0 + gate * (1.0 - sig))).astype(jnp.bfloat16)
    gup = (gh * gate * sig).astype(jnp.bfloat16)
    ggate_ref[...] = ggate
    gup_ref[...] = gup
    gm = plain_dot(ggate, wg_ref[...]) + plain_dot(gup, wu_ref[...])
    ratio, inverse = rms_parts(mid_ref[...])
    back, ggain = norm_back(gm, ratio, inverse, gain_ref[...])
    ggain_ref[...] = ggain
    gmid = gx + back
    gmid_ref[...] = gmid
    go_ref[...] = gmid.astype(jnp.bfloat16)


def attend_back_kernel(
    chunk_rows,
    go_ref,
    wo_ref,
    q_ref,
    win_ref,
    low_ref,
    high_ref,
    o_ref,
    lse_ref,
    gq_ref,
    gwin_ref,
    grad_ref,
    delta_ref,
    acc_ref,
):
    own = go_ref.shape[0]
    chunks = win_ref.shape[0] // chunk_rows
    go = go_ref[...]
    lane = lax.broadcasted_iota(jnp.int32, (GROUPS * own, TILE), 1)
    for j in range(KV):
        for g in range(GROUPS):
            grad_ref[j, g * own : (g + 1) * own, :] = rows_by_rows(
                go, wo_ref[j * GROUPS + g]
            ).astype(jnp.bfloat16)
        product = jnp.where(lane >= HD, grad_ref[j].astype(jnp.float32) * o_ref[j], 0.0)
        delta_ref[j] = jnp.sum(product.T, axis=0, keepdims=True)
    acc_ref[...] = jnp.zeros_like(acc_ref)

    def step(chunk, unused):
        allowed = allowed_pairs(chunk, chunk_rows, low_ref, high_ref)
        start = pl.multiple_of(chunk * chunk_rows, chunk_rows)
        for j in range(KV):
            tile = win_ref[pl.ds(start, chunk_rows), j * TILE : (j + 1) * TILE]
            queries = q_ref[j]
            grads = grad_ref[j]
            scores = rows_by_rows(tile, queries) - lse_ref[j]
            weights = jnp.exp(jnp.where(allowed, scores, MASKED))
            slopes = rows_by_rows(tile, grads) - delta_ref[j]
            score_grads = (weights * slopes).astype(jnp.bfloat16)
            acc_ref[j] += cols_by_cols(tile, score_grads)
            both = plain_dot(score_grads, queries) + plain_dot(
                weights.astype(jnp.bfloat16), grads
            )
            gwin_ref[pl.ds(start, chunk_rows), j * TILE : (j + 1) * TILE] = both.astype(
                jnp.bfloat16
            )
        return unused

    lax.fori_loop(0, chunks, step, 0)
    for j in range(KV):
        gq_ref[j] = (0.125 * acc_ref[j]).T


def project_back_kernel(
    gq_ref, gkv_ref, cq_ref, ckv_ref, sn_ref, w_ref, x_ref, gain_ref, gmid_ref, gqkv_ref, gx_ref, ggain_ref
):
    own = x_ref.shape[0]
    sines = -sn_ref[...]
    for head in range(H + KV):
        if head < H:
            rows = slice((head % GROUPS) * own, (head % GROUPS + 1) * own)
            lin = gq_ref[head // GROUPS, rows, :]
            cosines = cq_ref[...]
        else:
            lin = gkv_ref[:, (head - H) * TILE : (head - H + 1) * TILE]
            cosines = ckv_ref[...]
        turned = (lin * cosines + swap_halves(lin) * sines).astype(jnp.bfloat16)
        gqkv_ref[:, head * TILE : (head + 1) * TILE] = turned
    grad_normed = plain_dot(gqkv_ref[...], w_ref[...])
    ratio, inverse = rms_parts(x_ref[...])
    back, ggain = norm_back(grad_normed, ratio, inverse, gain_ref[...])
    ggain_ref[...] = ggain
    gx_ref[...] = gmid_ref[...] + back


def body(tokens, w_attn, attn_gain, w_gate, w_up, w_down, mlp_gain, seq_lengths, cotangent):
    own, width = tokens.shape
    layers = w_attn.shape[0]
    count = lax.axis_size("dp") * lax.axis_size("tensor")
    qkv_rows = (H + 2 * KV) * HD
    reach = min((L_MAX + own - 2) // own, count - 1)
    window_rows = (reach + 1) * own
    chunk_rows = 2 * own if (reach + 1) % 2 == 0 else own
    tiles = (H + KV) * TILE
    f32, bf16 = jnp.float32, jnp.bfloat16
    shape = jax.ShapeDtypeStruct

    seq_ends = jnp.cumsum(seq_lengths)
    starts = seq_ends - seq_lengths
    first_place = lax.axis_index(AXES) * own
    places = first_place + jnp.arange(own, dtype=jnp.int32)
    begin = sequence_start(places, starts)
    first_key = first_place - reach * own
    low = jnp.tile(begin - first_key, GROUPS)[None, :]
    high = jnp.tile(places - first_key, GROUPS)[None, :]
    frequencies = jnp.power(ROPE_BASE, -2.0 * jnp.arange(HD // 2, dtype=f32) / HD)
    angles = (places - begin).astype(f32)[:, None] * frequencies[None, :]
    cosines, sines = jnp.cos(angles), jnp.sin(angles)
    zeros, ones = jnp.zeros((own, HD), f32), jnp.ones((own, HD), f32)
    cos_q = jnp.concatenate([cosines, cosines, zeros], axis=1)
    cos_kv = jnp.concatenate([cosines, cosines, ones], axis=1)
    sin_all = jnp.concatenate([-sines, sines, zeros], axis=1)

    gate_all = lax.all_gather(w_gate, "tensor", axis=1, tiled=True)
    up_all = lax.all_gather(w_up, "tensor", axis=1, tiled=True)
    down_all = lax.all_gather(w_down, "tensor", axis=1, tiled=True)
    q_rows = w_attn[:, : H * HD].reshape(layers, H, HD, width)
    k_rows = w_attn[:, H * HD : (H + KV) * HD].reshape(layers, KV, HD, width)
    v_rows = w_attn[:, (H + KV) * HD : qkv_rows].reshape(layers, KV, HD, width)
    w_in = jnp.concatenate(
        [
            jnp.pad(q_rows, ((0, 0), (0, 0), (0, HD), (0, 0))),
            jnp.concatenate([k_rows, v_rows], axis=2),
        ],
        axis=1,
    ).reshape(layers, tiles, width)
    w_out = jnp.pad(
        jnp.swapaxes(w_attn[:, qkv_rows:], 1, 2).reshape(layers, H, HD, width),
        ((0, 0), (0, 0), (HD, 0), (0, 0)),
    )

    stream = tokens.astype(f32)
    stored = []
    for layer in range(layers):
        queries, kv_own, normed = call(
            project_kernel,
            (
                shape((KV, GROUPS * own, TILE), bf16),
                shape((own, KV * TILE), bf16),
                shape((own, width), bf16),
            ),
        )(stream, attn_gain[layer][None], w_in[layer], cos_q, cos_kv, sin_all)
        window = call(
            functools.partial(fetch_kernel, count, reach),
            shape((reach + 1, own, KV * TILE), bf16),
            [pltpu.SemaphoreType.DMA((reach,)), pltpu.SemaphoreType.DMA((reach,))],
            collective_id=0,
            has_side_effects=True,
        )(kv_own).reshape(window_rows, KV * TILE)
        hidden_rows = gate_all.shape[1]
        x_out, middle, normed_m, gate, up, hidden, mixed, lse = call(
            functools.partial(attend_kernel, chunk_rows),
            (
                shape((own, width), f32),
                shape((own, width), f32),
                shape((own, width), bf16),
                shape((own, hidden_rows), f32),
                shape((own, hidden_rows), f32),
                shape((own, hidden_rows), bf16),
                shape((KV, GROUPS * own, TILE), f32),
                shape((KV, 1, GROUPS * own), f32),
            ),
            [
                pltpu.VMEM((KV, TILE, GROUPS * own), f32),
                pltpu.VMEM((KV, 1, GROUPS * own), f32),
                pltpu.VMEM((KV, 1, GROUPS * own), f32),
            ],
        )(
            queries,
            window,
            low,
            high,
            stream,
            w_out[layer],
            mlp_gain[layer][None],
            gate_all[layer],
            up_all[layer],
            down_all[layer],
        )
        stored.append((stream, queries, normed, window, middle, normed_m, gate, up, hidden, mixed, lse))
        stream = x_out

    upstream = cotangent
    gains = []
    sums = []
    for layer in reversed(range(layers)):
        x_in, queries, normed, window, middle, normed_m, gate, up, hidden, mixed, lse = stored[layer]
        hidden_rows = gate_all.shape[1]
        gy, ggate, gup, gmid, go, gain_m = call(
            mlp_back_kernel,
            (
                shape((own, width), bf16),
                shape((own, hidden_rows), bf16),
                shape((own, hidden_rows), bf16),
                shape((own, width), f32),
                shape((own, width), bf16),
                shape((1, width), f32),
            ),
        )(
            upstream,
            middle,
            gate,
            up,
            mlp_gain[layer][None],
            gate_all[layer],
            up_all[layer],
            down_all[layer],
        )
        heads = jnp.transpose(
            mixed.reshape(H, own, TILE)[:, :, HD:].astype(bf16), (1, 0, 2)
        ).reshape(own, H * HD)
        gq, gwin = call(
            functools.partial(attend_back_kernel, chunk_rows),
            (
                shape((KV, GROUPS * own, TILE), f32),
                shape((window_rows, KV * TILE), bf16),
            ),
            [
                pltpu.VMEM((KV, GROUPS * own, TILE), bf16),
                pltpu.VMEM((KV, 1, GROUPS * own), f32),
                pltpu.VMEM((KV, TILE, GROUPS * own), f32),
            ],
        )(go, w_out[layer], queries, window, low, high, mixed, lse)
        gkv = call(
            functools.partial(return_kernel, count, reach),
            shape((own, KV * TILE), f32),
            [
                pltpu.VMEM((reach, own, KV * TILE), bf16),
                pltpu.SemaphoreType.DMA((reach,)),
                pltpu.SemaphoreType.DMA((reach,)),
            ],
            collective_id=1,
            has_side_effects=True,
        )(gwin.reshape(reach + 1, own, KV * TILE))
        gqkv, upstream, gain_a = call(
            project_back_kernel,
            (
                shape((own, tiles), bf16),
                shape((own, width), f32),
                shape((1, width), f32),
            ),
        )(gq, gkv, cos_q, cos_kv, sin_all, w_in[layer], x_in, attn_gain[layer][None], gmid)
        gains.append((gain_a, gain_m))

        def halves(part):
            return lax.psum_scatter(part.astype(bf16), "tensor", scatter_dimension=0, tiled=True)

        ffn = [cols_by_cols(ggate, normed_m), cols_by_cols(gup, normed_m), cols_by_cols(hidden, gy)]
        own_gate, own_up, own_down = [
            lax.psum_scatter(halves(part), "dp", scatter_dimension=0, tiled=True) for part in ffn
        ]
        g_out = cols_by_cols(go, heads)
        g_in = cols_by_cols(gqkv, normed).reshape(H + KV, 2, HD, width)
        attn_part = jnp.concatenate(
            [
                g_in[:H, 0].reshape(H * HD, width),
                g_in[H:, 0].reshape(KV * HD, width),
                g_in[H:, 1].reshape(KV * HD, width),
                g_out,
            ],
            axis=0,
        ).astype(bf16)
        own_attn = lax.psum_scatter(attn_part, AXES, scatter_dimension=0, tiled=True)
        sums.append([value.astype(f32) for value in (own_attn, own_gate, own_up, own_down)])
    gains = gains[::-1]
    sums = sums[::-1]
    gain_sums = lax.psum(
        jnp.concatenate([row for pair in gains for row in pair], axis=0), AXES
    )
    attn_sum, gate_sum, up_sum, down_sum = [
        jnp.stack([entry[slot] for entry in sums], axis=0) for slot in range(4)
    ]
    return (
        stream,
        upstream,
        attn_sum,
        gain_sums[0::2],
        gate_sum,
        up_sum,
        down_sum,
        gain_sums[1::2],
    )


def solution(mesh):
    placed = (
        P(AXES, None),
        P(),
        P(),
        P(None, "tensor", None),
        P(None, "tensor", None),
        P(None, "tensor", None),
        P(),
        P(),
        P(AXES, None),
    )
    return jax.shard_map(
        body,
        mesh=mesh,
        in_specs=placed,
        out_specs=(
            P(AXES, None),
            P(AXES, None),
            P(None, AXES, None),
            P(),
            P(None, ("tensor", "dp"), None),
            P(None, ("tensor", "dp"), None),
            P(None, ("tensor", "dp"), None),
            P(),
        ),
        check_vma=False,
    )
```

time: 1250 us -> 1380 us (1.10)
  Pallas kernels: 0 us -> 266 us
  waiting for transfers between devices: 647 us -> 888 us
  starting transfers between devices: 146 us -> 0.71 us
  matrix products: 126 us -> 16.6 us
  other arithmetic: 95.2 us -> 9.88 us
  local copies, waits for them, and re-layouts: 116 us -> 88.3 us
    unnamed x8 -> x25, waiting for transfers between devices: 436 us -> 888 us
    pallas_call x0 -> x14, Pallas kernels: none -> 266 us  [the longest x2 89 us: body(): call(functools.partial(return_kernel, count, reach), shape((own, KV * TIL...]
    ppermute x44 -> x0, starting transfers between devices: 145 us -> none  [passed_along(): return lax.ppermute(array, axis, pairs)]
    ppermute x44 -> x0, waiting for transfers between devices: 136 us -> none  [passed_along(): return lax.ppermute(array, axis, pairs)]
    dot_general x42 -> x10, matrix products: 126 us -> 16.6 us  [cols_by_cols(): lax.dot_general(left, right, (((0,), (0,)), ((), ())), preferred_element_...]
    reduce_scatter x4 -> x6, waiting for transfers between devices: 76.1 us -> 0.11 us  [halves(): lax.psum_scatter(part.astype(bf16), 'tensor', scatter_dimension=0, tiled=...]
    all_gather x4 -> x0, blocking collectives: 32.7 us -> none  [the longest x2 24 us: body(): gathered = lax.all_gather(normed_m, 'tensor', axis=0, tiled=True)]
    psum x1, blocking collectives: 59.3 us -> 88.2 us  [body(): lax.psum(jnp.concatenate([row for pair in gains for row in pair], axis=0)...]
  transfers between devices with their start and end apart: 50 -> 17, of which waited for: 50 -> 8; matrix products, arithmetic and copies ran while one was open for 4% -> 7% of each run, Pallas kernels for 0% -> 7%
where the time goes in v1:
time: 1380 us; the launch traced here: 1370 us
  waiting for transfers between devices  888 us (64%)
  Pallas kernels  266 us (19%)
  local copies, waits for them, and re-layouts  88.3 us (6%)
  blocking collectives  88.2 us (6%)
  matrix products  16.6 us (1%)
  between operations  15 us (1%)
    unnamed x25, waiting for transfers between devices  888 us
    pallas_call x2, Pallas kernels, body(): call(functools.partial(return_kernel, count, reach), shape((own, KV * TIL...  89 us
    psum x1, blocking collectives, body(): lax.psum(jnp.concatenate([row for pair in gains for row in pair], axis=0)...  88.2 us
    pallas_call x2, Pallas kernels, body(): call(functools.partial(fetch_kernel, count, reach), shape((reach + 1, own...  66.3 us
    pallas_call x2, Pallas kernels, body(): call(functools.partial(attend_kernel, chunk_rows), (shape((own, width), f...  41.4 us
    unnamed x78, local copies, waits for them, and re-layouts  40.4 us
    pallas_call x2, Pallas kernels, body(): call(functools.partial(attend_back_kernel, chunk_rows), (shape((KV, GROUP...  38.7 us
  transfers between devices with their start and end apart: 17, of which 8 were waited for; matrix products, arithmetic and copies ran while one was open for 7% of the time, Pallas kernels for 7%

profile of v1, /device:TPU:0, one launch (start us, length us, event | category | flops | bytes accessed | tf_op | source)
XLA Modules:
  0.0 1372.8 jit_solution(8126868407699351794)
XLA Ops:
  7.2 4.0 copy.79
  16.1 2.6 fusion.9
  18.7 2.6 fusion.10
  37.2 4.1 shard_map.152
  41.3 20.1 %shard_map.153 = bf16[12,192,384]{2,1,0:T(8,128)(2,1)} custom-call(bf16[192,384]{1,0:T(8,128)(2,1)} %get-tuple-element.53.own_ref), custom_call_target="tpu_custom_call" | custom-call | tf_op jit(solution)/shard_map/pallas_call | solution.py:428
  65.3 4.4 slice_bitcast_fusion
  69.7 4.5 slice_bitcast_fusion.1
  74.2 4.4 slice_bitcast_fusion.2
  78.7 20.7 %shard_map.154 = (f32[192,576]{1,0:T(8,128)}, f32[192,576]{1,0:T(8,128)}, bf16[192,576]{1,0:T(8,128)(2,1)}, f32[192,1536]{1,0:T(8,128)}, f32[192,1536]{1,0:T(8,1...) custom-call(bf16[3,576,128]{2,1,0:T(8,128)(2,1)} %get-tuple-element.52.q_ref, ...), custom_call_target="tpu_custom_call" | custom-call | tf_op jit(solution)/shard_map/pallas_call | solution.py:436
  99.4 3.7 shard_map.155
  103.0 46.2 %shard_map.156 = bf16[12,192,384]{2,1,0:T(8,128)(2,1)} custom-call(bf16[192,384]{1,0:T(8,128)(2,1)} %get-tuple-element.56.own_ref), custom_call_target="tpu_custom_call" | custom-call | tf_op jit(solution)/shard_map/pallas_call | solution.py:428
  149.2 20.7 %shard_map.157 = (f32[192,576]{1,0:T(8,128)}, f32[192,576]{1,0:T(8,128)}, bf16[192,576]{1,0:T(8,128)(2,1)}, f32[192,1536]{1,0:T(8,128)}, f32[192,1536]{1,0:T(8,1...) custom-call(bf16[3,576,128]{2,1,0:T(8,128)(2,1)} %get-tuple-element.55.q_ref, ...), custom_call_target="tpu_custom_call" | custom-call | tf_op jit(solution)/shard_map/pallas_call | solution.py:436
  169.9 6.7 shard_map.158
  176.6 19.4 %shard_map.159 = (f32[3,576,128]{2,1,0:T(8,128)}, bf16[2304,384]{1,0:T(8,128)(2,1)}) custom-call(bf16[192,576]{1,0:T(8,128)(2,1)} %get-tuple-element.61.go_ref, bf16[9,128,576]{2,1,0:T(8,128)(2,1)} %get-tuple-element.128.wo_ref, bf16[3,576,128]{2,1,0:T(8,128)(2,1)} %get-tuple-element.55.q_ref, bf16[2304,384]{1,0:T(8,128)(2,1)} %bitcast.90, ...), custom_call_target="tpu_custom_call" | custom-call | tf_op jit(solution)/shard_map/pallas_call | solution.py:497
  196.0 45.6 %shard_map.160.gkv_ref = f32[192,384]{1,0:T(8,128)} custom-call(bf16[12,192,384]{2,1,0:T(8,128)(2,1)} %bitcast.102), custom_call_target="tpu_custom_call" | custom-call | tf_op jit(solution)/shard_map/pallas_call | solution.py:509
  241.6 4.3 shard_map.161
  245.9 6.8 shard_map.162
  252.7 2.9 convolution_convert_fusion.1
  265.9 19.3 %shard_map.163 = (f32[3,576,128]{2,1,0:T(8,128)}, bf16[2304,384]{1,0:T(8,128)(2,1)}) custom-call(bf16[192,576]{1,0:T(8,128)(2,1)} %get-tuple-element.71.go_ref, bf16[9,128,576]{2,1,0:T(8,128)(2,1)} %get-tuple-element.129.wo_ref, bf16[3,576,128]{2,1,0:T(8,128)(2,1)} %get-tuple-element.52.q_ref, bf16[2304,384]{1,0:T(8,128)(2,1)} %bitcast.88, ...), custom_call_target="tpu_custom_call" | custom-call | tf_op jit(solution)/shard_map/pallas_call | solution.py:497
  285.2 43.4 %shard_map.164.gkv_ref = f32[192,384]{1,0:T(8,128)} custom-call(bf16[12,192,384]{2,1,0:T(8,128)(2,1)} %bitcast.101), custom_call_target="tpu_custom_call" | custom-call | tf_op jit(solution)/shard_map/pallas_call | solution.py:509
  329.0 4.9 shard_map.165
  342.8 2.6 concatenate.31
  357.5 2.6 concatenate.32
  376.6 88.2 %psum.7 = f32[4,576]{1,0:T(4,128)S(1)} all-reduce(f32[4,576]{1,0:T(4,128)S(1)} %pad_maximum_fusion.1), channel_id=1, replica_groups=mesh['dp'=16,'tensor'=2] {'dp','tensor'}, use_global_device_ids=true, to_apply=%region_4.5 | all-reduce | flops 2304 | bytes 18432 | tf_op jit(solution)/shard_map/psum | solution.py:552
  466.0 27.7 %reduce-scatter.43.cloned.1.call-done = bf16[48,576]{1,0:T(8,128)(2,1)} async-done(((bf16[1536,576]{1,0:T(8,128)(2,1)}), bf16[48,576]{1,0:T(8,128)(2,1)}) %reduce-scatter.43.cloned.1.call-update) | async-done | bytes 55312
  494.8 101.2 %reduce-scatter.45.cloned.1.call-done = bf16[48,576]{1,0:T(8,128)(2,1)} async-done(((bf16[1536,576]{1,0:T(8,128)(2,1)}), bf16[48,576]{1,0:T(8,128)(2,1)}) %reduce-scatter.45.cloned.1.call-update) | async-done | bytes 55312
  597.8 125.9 %reduce-scatter.55.cloned.1.call-done = bf16[48,576]{1,0:T(8,128)(2,1)} async-done(((bf16[768,576]{1,0:T(8,128)(2,1)}), bf16[48,576]{1,0:T(8,128)(2,1)}) %reduce-scatter.55.cloned.1.call-update) | async-done | bytes 55312
  724.9 126.9 %reduce-scatter.57.cloned.1.call-done = bf16[48,576]{1,0:T(8,128)(2,1)} async-done(((bf16[768,576]{1,0:T(8,128)(2,1)}), bf16[48,576]{1,0:T(8,128)(2,1)}) %reduce-scatter.57.cloned.1.call-update) | async-done | bytes 55312
  852.9 126.6 %reduce-scatter.51.cloned.1.call-done = bf16[48,576]{1,0:T(8,128)(2,1)} async-done(((bf16[768,576]{1,0:T(8,128)(2,1)}), bf16[48,576]{1,0:T(8,128)(2,1)}) %reduce-scatter.51.cloned.1.call-update) | async-done | bytes 55312
  980.6 126.6 %reduce-scatter.53.cloned.1.call-done = bf16[48,576]{1,0:T(8,128)(2,1)} async-done(((bf16[768,576]{1,0:T(8,128)(2,1)}), bf16[48,576]{1,0:T(8,128)(2,1)}) %reduce-scatter.53.cloned.1.call-update) | async-done | bytes 55312
  1108.3 126.6 %reduce-scatter.47.cloned.1.call-done = bf16[48,576]{1,0:T(8,128)(2,1)} async-done(((bf16[768,576]{1,0:T(8,128)(2,1)}), bf16[48,576]{1,0:T(8,128)(2,1)}) %reduce-scatter.47.cloned.1.call-update) | async-done | bytes 55312
  1236.0 126.6 %reduce-scatter.49.cloned.1.call-done = bf16[48,576]{1,0:T(8,128)(2,1)} async-done(((bf16[768,576]{1,0:T(8,128)(2,1)}), bf16[48,576]{1,0:T(8,128)(2,1)}) %reduce-scatter.49.cloned.1.call-update) | async-done | bytes 55312
  (182 shorter events, 85.2 us)
Async XLA Ops:
  7.2 4.2 copy-start.5
  7.2 58.1 %all-gather.8.cloned.1.call-start = ((), (), s32[]{:S(2)}) async-start(), calls=%async_computation.16 | async-start | bytes 5898240 | tf_op jit(solution)/shard_map/all_gather | solution.py:401
  11.3 2.5 copy-start.6
  11.3 58.4 %all-gather.6.cloned.1.call-start = ((), (), s32[]{:S(2)}) async-start(), calls=%async_computation.15 | async-start | bytes 5898240 | tf_op jit(solution)/shard_map/all_gather | solution.py:400
  13.7 60.5 %all-gather.4.cloned.1.call-start = ((), (), s32[]{:S(2)}) async-start(), calls=%async_computation.14 | async-start | bytes 5898240 | tf_op jit(solution)/shard_map/all_gather | solution.py:399
  16.1 346.4 %reduce-scatter.39.cloned.1.call-start = ((), (), s32[]{:S(2)}) async-start(), calls=%async_computation.21 | async-start | bytes 2654208 | tf_op jit(solution)/shard_map/reduce_scatter | solution.py:531
  18.7 2.6 copy-start.26
  25.3 5.8 copy-start.20
  25.3 9.0 copy-start
  28.5 5.8 copy-start.3
  28.5 5.8 copy-start.4
  245.9 6.8 copy-start.14
  252.7 3.0 copy-start.15
  252.7 3.0 copy-start.19
  255.6 109.2 %reduce-scatter.41.cloned.1.call-start = ((), (), s32[]{:S(2)}) async-start(), calls=%async_computation.22 | async-start | bytes 2654208 | tf_op jit(solution)/shard_map/reduce_scatter | solution.py:531
  257.6 109.6 %reduce-scatter.35.cloned.1.call-start = ((), (), s32[]{:S(2)}) async-start(), calls=%async_computation.19 | async-start | bytes 2654208 | tf_op jit(solution)/shard_map/reduce_scatter | solution.py:531
  259.6 109.9 %reduce-scatter.37.cloned.1.call-start = ((), (), s32[]{:S(2)}) async-start(), calls=%async_computation.20 | async-start | bytes 2654208 | tf_op jit(solution)/shard_map/reduce_scatter | solution.py:531
  261.7 110.2 %reduce-scatter.31.cloned.1.call-start = ((), (), s32[]{:S(2)}) async-start(), calls=%async_computation.17 | async-start | bytes 2654208 | tf_op jit(solution)/shard_map/reduce_scatter | solution.py:531
  263.7 110.6 %reduce-scatter.33.cloned.1.call-start = ((), (), s32[]{:S(2)}) async-start(), calls=%async_computation.18 | async-start | bytes 2654208 | tf_op jit(solution)/shard_map/reduce_scatter | solution.py:531
  265.7 228.0 %reduce-scatter.43.cloned.1.call-start = ((), (), s32[]{:S(2)}) async-start(), calls=%async_computation.23 | async-start | bytes 2027520
  329.0 4.9 copy-start.18
  339.2 3.2 copy-start.8
  345.4 2.4 copy-start.1
  347.7 248.3 %reduce-scatter.45.cloned.1.call-start = ((), (), s32[]{:S(2)}) async-start(), calls=%async_computation.24 | async-start | bytes 2027520
  353.9 3.3 copy-start.7
  362.4 361.3 %reduce-scatter.55.cloned.1.call-start = ((), (), s32[]{:S(2)}) async-start(), calls=%async_computation.29 | async-start | bytes 1044480
  364.8 487.0 %reduce-scatter.57.cloned.1.call-start = ((), (), s32[]{:S(2)}) async-start(), calls=%async_computation.30 | async-start | bytes 1044480
  367.1 612.3 %reduce-scatter.51.cloned.1.call-start = ((), (), s32[]{:S(2)}) async-start(), calls=%async_computation.27 | async-start | bytes 1044480
  369.5 737.7 %reduce-scatter.53.cloned.1.call-start = ((), (), s32[]{:S(2)}) async-start(), calls=%async_computation.28 | async-start | bytes 1044480
  371.9 863.0 %reduce-scatter.47.cloned.1.call-start = ((), (), s32[]{:S(2)}) async-start(), calls=%async_computation.25 | async-start | bytes 1044480
  374.2 2.4 copy-start.25
  374.2 988.4 %reduce-scatter.49.cloned.1.call-start = ((), (), s32[]{:S(2)}) async-start(), calls=%async_computation.26 | async-start | bytes 1044480
  (12 other events, 24.3 us)
Sparse Core Ops, SparseCore 0:
  11.4 15.9 all-gather.7
  29.0 14.4 all-gather.5
  45.0 14.4 all-gather.3
  255.7 52.4 reduce-scatter.38
  310.4 10.4 reduce-scatter.40
  323.0 10.4 reduce-scatter.34
  335.8 10.4 reduce-scatter.36
  348.6 10.4 reduce-scatter.30
  361.4 10.4 reduce-scatter.32
  377.0 116.6 reduce-scatter.42
  499.0 96.9 reduce-scatter.44
  600.6 123.1 reduce-scatter.54
  728.5 123.1 reduce-scatter.56
  856.3 123.0 reduce-scatter.50
  984.0 123.0 reduce-scatter.52
  1111.8 123.0 reduce-scatter.46
  1239.5 123.0 reduce-scatter.48

commit v2 on v1

--- a/solution.py
+++ b/solution.py
@@ -366,6 +366,202 @@
     back, ggain = norm_back(grad_normed, ratio, inverse, gain_ref[...])
     ggain_ref[...] = ggain
     gx_ref[...] = gmid_ref[...] + back
+
+
+def sum_kernel(sizes, orders, *refs):
+    parts = len(orders)
+    pair, across, up, deep = sizes
+    core = lax.axis_index("tensor")
+    index = lax.axis_index("dp")
+    place = {
+        "t": core,
+        "x": lax.rem(index, across),
+        "y": lax.rem(lax.div(index, across), up),
+        "z": lax.div(index, across * up),
+    }
+    extent = {"t": pair, "x": across, "y": up, "z": deep}
+    stages = len(orders[0])
+    steps = max(extent.values())
+    ins, gain_ref = refs[:parts], refs[parts]
+    outs, gain_out = refs[parts + 1 : 2 * parts + 1], refs[2 * parts + 1]
+    rest = list(refs[2 * parts + 2 :])
+    kept = [[rest.pop(0) for _ in range(stages - 1)] for _ in range(parts)]
+    held = [[rest.pop(0) for _ in range(stages)] for _ in range(parts)]
+    gain_held = [rest.pop(0) for _ in range(stages)]
+    gain_sum = rest.pop(0)
+    send_sem, recv_sem, gain_send, gain_recv = rest
+
+    def partner(axis, coordinate):
+        at = dict(place)
+        at[axis] = coordinate
+        return {"dp": (at["z"] * up + at["y"]) * across + at["x"], "tensor": at["t"]}
+
+    barrier = pltpu.get_barrier_semaphore()
+    partners = 0
+    for axis, size in extent.items():
+        for by in range(1, size):
+            partners += 1
+            pl.semaphore_signal(
+                barrier,
+                inc=1,
+                device_id=partner(axis, lax.rem(place[axis] + by, size)),
+                device_id_type=MESH,
+            )
+    pl.semaphore_wait(barrier, partners)
+
+    def copies(part, stage):
+        axis = orders[part][stage]
+        size = extent[axis]
+        source = ins[part] if stage == 0 else kept[part][stage - 1]
+        blocks = source.shape[0] // size
+        made = []
+        for by in range(1, size):
+            target = lax.rem(place[axis] + by, size)
+            made.append(
+                pltpu.make_async_remote_copy(
+                    src_ref=source.at[pl.ds(target * blocks, blocks)],
+                    dst_ref=held[part][stage].at[pl.ds((by - 1) * blocks, blocks)],
+                    send_sem=send_sem.at[(part * stages + stage) * steps + by],
+                    recv_sem=recv_sem.at[(part * stages + stage) * steps + by],
+                    device_id=partner(axis, target),
+                    device_id_type=MESH,
+                )
+            )
+        return made
+
+    def gain_copies(stage):
+        axis = orders[0][stage]
+        size = extent[axis]
+        return [
+            pltpu.make_async_remote_copy(
+                src_ref=gain_ref if stage == 0 else gain_sum.at[stage - 1],
+                dst_ref=gain_held[stage].at[place[axis]],
+                send_sem=gain_send.at[stage * steps + by],
+                recv_sem=gain_recv.at[stage * steps + by],
+                device_id=partner(axis, lax.rem(place[axis] + by, size)),
+                device_id_type=MESH,
+            )
+            for by in range(1, size)
+        ]
+
+    def start(part, stage):
+        for copy in copies(part, stage):
+            copy.start()
+
+    def finish(part, stage):
+        for copy in copies(part, stage):
+            copy.wait_recv()
+        axis = orders[part][stage]
+        size = extent[axis]
+        source = ins[part] if stage == 0 else kept[part][stage - 1]
+        blocks = source.shape[0] // size
+
+        def add(block, unused):
+            value = source[place[axis] * blocks + block].astype(jnp.float32)
+            for by in range(1, size):
+                value += held[part][stage][(by - 1) * blocks + block].astype(jnp.float32)
+            if stage < stages - 1:
+                kept[part][stage][block] = value.astype(jnp.bfloat16)
+            else:
+                outs[part][...] = value
+            return unused
+
+        lax.fori_loop(0, blocks, add, 0)
+
+    def start_gain(stage):
+        for copy in gain_copies(stage):
+            copy.start()
+
+    def finish_gain(stage):
+        axis = orders[0][stage]
+        for by, copy in enumerate(gain_copies(stage)):
+            copy.wait_recv()
+        gain_held[stage][place[axis]] = gain_ref[...] if stage == 0 else gain_sum[stage - 1]
+        value = gain_held[stage][0]
+        for other in range(1, extent[axis]):
+            value += gain_held[stage][other]
+        gain_sum[stage] = value
+
+    for part in range(parts):
+        start(part, 0)
+    start_gain(0)
+    for stage in range(stages):
+        for part in range(parts):
+            finish(part, stage)
+            if stage < stages - 1:
+                start(part, stage + 1)
+        finish_gain(stage)
+        if stage < stages - 1:
+            start_gain(stage + 1)
+    gain_out[...] = gain_sum[stages - 1]
+    for stage in range(stages):
+        for part in range(parts):
+            for copy in copies(part, stage):
+                copy.wait_send()
+        for copy in gain_copies(stage):
+            copy.wait_send()
+
+
+def directions(count):
+    side = round((count // 2) ** (1 / 3))
+    if side > 0 and 2 * side * side * side == count:
+        return side, side, 2 * side
+    return 1, 1, count
+
+
+def sum_grads(layer_parts, gains):
+    bf16 = jnp.bfloat16
+    pair = lax.axis_size("tensor")
+    across, up, deep = directions(lax.axis_size("dp"))
+    extent = {"t": pair, "x": across, "y": up, "z": deep}
+    width = gains.shape[1]
+    orders = ["txyz" if part % 2 == 0 else "tyxz" for part in range(len(layer_parts))]
+    chips = across * up * deep
+    stacked = []
+    for order, (attn, *ffn) in zip(orders, layer_parts):
+        pieces = attn.shape[0] // (chips * pair)
+        split = [jnp.transpose(attn.reshape(chips, pair, pieces, width), (1, 0, 2, 3))]
+        split += [part.reshape(pair, chips, pieces, width) for part in ffn]
+        whole = jnp.stack(split, axis=2).reshape(
+            pair, deep, up, across, len(split) * pieces, width
+        )
+        turn = (0, 3, 2, 1, 4, 5) if order == "txyz" else (0, 2, 3, 1, 4, 5)
+        stacked.append(
+            jnp.transpose(whole, turn).reshape(pair * chips, len(split) * pieces, width)
+        )
+    rows = stacked[0].shape[1]
+    stages = 4
+    kept, held = [], []
+    for order in orders:
+        blocks = pair * chips
+        for stage, axis in enumerate(order):
+            blocks //= extent[axis]
+            if stage < stages - 1:
+                kept.append(pltpu.VMEM((blocks, rows, width), bf16))
+            held.append(
+                pltpu.VMEM((max(extent[axis] - 1, 1) * blocks, rows, width), bf16)
+            )
+    gain_held = [pltpu.VMEM((extent[axis],) + gains.shape, jnp.float32) for axis in orders[0]]
+    steps = max(extent.values())
+    slots = len(orders) * stages * steps
+    *sums, gain_sums = call(
+        functools.partial(sum_kernel, (pair, across, up, deep), tuple(orders)),
+        tuple(jax.ShapeDtypeStruct((rows, width), jnp.float32) for _ in orders)
+        + (jax.ShapeDtypeStruct(gains.shape, jnp.float32),),
+        kept
+        + held
+        + gain_held
+        + [
+            pltpu.VMEM((stages,) + gains.shape, jnp.float32),
+            pltpu.SemaphoreType.DMA((slots,)),
+            pltpu.SemaphoreType.DMA((slots,)),
+            pltpu.SemaphoreType.DMA((stages * steps,)),
+            pltpu.SemaphoreType.DMA((stages * steps,)),
+        ],
+        collective_id=2,
+        has_side_effects=True,
+    )(*stacked, gains)
+    return [jnp.split(value, 4, axis=0) for value in sums], gain_sums
 
 
 def body(tokens, w_attn, attn_gain, w_gate, w_up, w_down, mlp_gain, seq_lengths, cotangent):
@@ -467,7 +663,7 @@
 
     upstream = cotangent
     gains = []
-    sums = []
+    parts = []
     for layer in reversed(range(layers)):
         x_in, queries, normed, window, middle, normed_m, gate, up, hidden, mixed, lse = stored[layer]
         hidden_rows = gate_all.shape[1]
@@ -527,12 +723,9 @@
         )(gq, gkv, cos_q, cos_kv, sin_all, w_in[layer], x_in, attn_gain[layer][None], gmid)
         gains.append((gain_a, gain_m))
 
-        def halves(part):
-            return lax.psum_scatter(part.astype(bf16), "tensor", scatter_dimension=0, tiled=True)
-
-        ffn = [cols_by_cols(ggate, normed_m), cols_by_cols(gup, normed_m), cols_by_cols(hidden, gy)]
-        own_gate, own_up, own_down = [
-            lax.psum_scatter(halves(part), "dp", scatter_dimension=0, tiled=True) for part in ffn
+        ffn = [
+            cols_by_cols(left, right).astype(bf16)
+            for left, right in ((ggate, normed_m), (gup, normed_m), (hidden, gy))
         ]
         g_out = cols_by_cols(go, heads)
         g_in = cols_by_cols(gqkv, normed).reshape(H + KV, 2, HD, width)
@@ -545,16 +738,14 @@
             ],
             axis=0,
         ).astype(bf16)
-        own_attn = lax.psum_scatter(attn_part, AXES, scatter_dimension=0, tiled=True)
-        sums.append([value.astype(f32) for value in (own_attn, own_gate, own_up, own_down)])
-    gains = gains[::-1]
-    sums = sums[::-1]
-    gain_sums = lax.psum(
-        jnp.concatenate([row for pair in gains for row in pair], axis=0), AXES
-    )
+        parts.append([attn_part, *ffn])
+    rows = [row for pair in gains[::-1] for row in pair]
+    rows.append(jnp.zeros((-len(rows) % 8, width), f32))
+    sums, gain_sums = sum_grads(parts[::-1], jnp.concatenate(rows, axis=0))
     attn_sum, gate_sum, up_sum, down_sum = [
         jnp.stack([entry[slot] for entry in sums], axis=0) for slot in range(4)
     ]
+    gain_sums = gain_sums[: 2 * layers]
     return (
         stream,
         upstream,

time: 1380 us -> 624 us (0.45)
  waiting for transfers between devices: 888 us -> 0.05 us
  Pallas kernels: 266 us -> 441 us
  blocking collectives: 88.2 us -> 0 us
  local copies, waits for them, and re-layouts: 88.3 us -> 122 us
    unnamed x25 -> x3, waiting for transfers between devices: 888 us -> 0.05 us
    pallas_call x0 -> x1, Pallas kernels: none -> 176 us  [sum_grads(): call(functools.partial(sum_kernel, (pair, across, up, deep), tuple(orders...]
    psum x1 -> x0, blocking collectives: 88.2 us -> none  [body(): lax.psum(jnp.concatenate([row for pair in gains for row in pair], axis=0)...]
    unnamed x78 -> x64, local copies, waits for them, and re-layouts: 40.4 us -> 14.8 us
    convert_element_type x0 -> x6, local copies, waits for them, and re-layouts: none -> 22.7 us  [body(): cols_by_cols(left, right).astype(bf16)]
    transpose x0 -> x2, local copies, waits for them, and re-layouts: none -> 14.5 us  [sum_grads(): jnp.transpose(whole, turn).reshape(pair * chips, len(split) * pieces, width)]
  transfers between devices with their start and end apart: 17 -> 3, of which waited for: 8 -> 0; matrix products, arithmetic and copies ran while one was open for 7% -> 6% of each run, Pallas kernels for 7% -> 4%
where the time goes in v2:
time: 624 us; the launch traced here: 613 us
  Pallas kernels  441 us (71%)
  local copies, waits for them, and re-layouts  122 us (20%)
  other arithmetic  19.3 us (3%)
  matrix products  16.7 us (3%)
  between operations  14.4 us (2%)
    pallas_call x1, Pallas kernels, sum_grads(): call(functools.partial(sum_kernel, (pair, across, up, deep), tuple(orders...  176 us
    pallas_call x2, Pallas kernels, body(): call(functools.partial(return_kernel, count, reach), shape((own, KV * TIL...  88.7 us
    pallas_call x2, Pallas kernels, body(): call(functools.partial(fetch_kernel, count, reach), shape((reach + 1, own...  66.3 us
    pallas_call x2, Pallas kernels, body(): call(functools.partial(attend_kernel, chunk_rows), (shape((own, width), f...  41.4 us
    pallas_call x2, Pallas kernels, body(): call(functools.partial(attend_back_kernel, chunk_rows), (shape((KV, GROUP...  38.8 us
    convert_element_type x6, local copies, waits for them, and re-layouts, body(): cols_by_cols(left, right).astype(bf16)  22.7 us
    dot_general x10, matrix products, cols_by_cols(): lax.dot_general(left, right, (((0,), (0,)), ((), ())), preferred_element_...  16.7 us
    unnamed x64, local copies, waits for them, and re-layouts  14.8 us
  transfers between devices with their start and end apart: 3, of which 0 were waited for; matrix products, arithmetic and copies ran while one was open for 6% of the time, Pallas kernels for 4%

profile of v2, /device:TPU:0, one launch (start us, length us, event | category | flops | bytes accessed | tf_op | source)
XLA Modules:
  0.0 613.4 jit_solution(2098915324162210250)
XLA Ops:
  7.2 4.0 copy.68
  37.1 4.1 shard_map.152
  41.1 20.1 %shard_map.153 = bf16[12,192,384]{2,1,0:T(8,128)(2,1)} custom-call(bf16[192,384]{1,0:T(8,128)(2,1)} %get-tuple-element.56.own_ref), custom_call_target="tpu_custom_call" | custom-call | tf_op jit(solution)/shard_map/pallas_call | solution.py:624
  65.2 4.4 slice_bitcast_fusion
  69.6 4.4 slice_bitcast_fusion.1
  74.0 4.3 slice_bitcast_fusion.2
  78.3 20.7 %shard_map.154 = (f32[192,576]{1,0:T(8,128)}, f32[192,576]{1,0:T(8,128)}, bf16[192,576]{1,0:T(8,128)(2,1)}, f32[192,1536]{1,0:T(8,128)}, f32[192,1536]{1,0:T(8,1...) custom-call(bf16[3,576,128]{2,1,0:T(8,128)(2,1)} %get-tuple-element.55.q_ref, ...), custom_call_target="tpu_custom_call" | custom-call | tf_op jit(solution)/shard_map/pallas_call | solution.py:632
  99.0 3.7 shard_map.155
  102.7 46.2 %shard_map.156 = bf16[12,192,384]{2,1,0:T(8,128)(2,1)} custom-call(bf16[192,384]{1,0:T(8,128)(2,1)} %get-tuple-element.59.own_ref), custom_call_target="tpu_custom_call" | custom-call | tf_op jit(solution)/shard_map/pallas_call | solution.py:624
  148.9 20.7 %shard_map.157 = (f32[192,576]{1,0:T(8,128)}, f32[192,576]{1,0:T(8,128)}, bf16[192,576]{1,0:T(8,128)(2,1)}, f32[192,1536]{1,0:T(8,128)}, f32[192,1536]{1,0:T(8,1...) custom-call(bf16[3,576,128]{2,1,0:T(8,128)(2,1)} %get-tuple-element.58.q_ref, ...), custom_call_target="tpu_custom_call" | custom-call | tf_op jit(solution)/shard_map/pallas_call | solution.py:632
  170.8 6.7 %shard_map.158 = (bf16[192,576]{1,0:T(8,128)(2,1)}, bf16[192,1536]{1,0:T(8,128)(2,1)}, bf16[192,1536]{1,0:T(8,128)(2,1)}, f32[192,576]{1,0:T(8,128)}, bf16[192,576]{1,0:T(8,128)(2,1)}, /*index=5*/f32[1,576]{1,0:T(1,128)}) custom-call(bf16[192,576]{1,0:T(8,128)(2,1)} %gx_ref.1, f32[192,576]{1,0:T(8,128)} %get-tuple-element.61.mid_ref, ...), custom_call_target="tpu_custom_call" | custom-call | tf_op jit(solution)/shard_map/pallas_call | solution.py:670
  177.5 19.4 %shard_map.159 = (f32[3,576,128]{2,1,0:T(8,128)}, bf16[2304,384]{1,0:T(8,128)(2,1)}) custom-call(bf16[192,576]{1,0:T(8,128)(2,1)} %get-tuple-element.64.go_ref, bf16[9,128,576]{2,1,0:T(8,128)(2,1)} %get-tuple-element.118.wo_ref, bf16[3,576,128]{2,1,0:T(8,128)(2,1)} %get-tuple-element.58.q_ref, bf16[2304,384]{1,0:T(8,128)(2,1)} %bitcast.118, ...), custom_call_target="tpu_custom_call" | custom-call | tf_op jit(solution)/shard_map/pallas_call | solution.py:693
  196.9 45.8 %shard_map.160.gkv_ref = f32[192,384]{1,0:T(8,128)} custom-call(bf16[12,192,384]{2,1,0:T(8,128)(2,1)} %bitcast.138), custom_call_target="tpu_custom_call" | custom-call | tf_op jit(solution)/shard_map/pallas_call | solution.py:705
  242.8 4.3 shard_map.161
  255.0 6.7 %shard_map.162 = (bf16[192,576]{1,0:T(8,128)(2,1)}, bf16[192,1536]{1,0:T(8,128)(2,1)}, bf16[192,1536]{1,0:T(8,128)(2,1)}, f32[192,576]{1,0:T(8,128)}, bf16[192,576]{1,0:T(8,128)(2,1)}, /*index=5*/f32[1,576]{1,0:T(1,128)}) custom-call(f32[192,576]{1,0:T(8,128)} %get-tuple-element.70.gx_ref, f32[192,576]{1,0:T(8,128)} %get-tuple-element.71.mid_ref, ...), custom_call_target="tpu_custom_call" | custom-call | tf_op jit(solution)/shard_map/pallas_call | solution.py:670
  261.7 19.4 %shard_map.163 = (f32[3,576,128]{2,1,0:T(8,128)}, bf16[2304,384]{1,0:T(8,128)(2,1)}) custom-call(bf16[192,576]{1,0:T(8,128)(2,1)} %get-tuple-element.74.go_ref, bf16[9,128,576]{2,1,0:T(8,128)(2,1)} %get-tuple-element.119.wo_ref, bf16[3,576,128]{2,1,0:T(8,128)(2,1)} %get-tuple-element.55.q_ref, bf16[2304,384]{1,0:T(8,128)(2,1)} %bitcast.116, ...), custom_call_target="tpu_custom_call" | custom-call | tf_op jit(solution)/shard_map/pallas_call | solution.py:693
  281.1 42.9 %shard_map.164.gkv_ref = f32[192,384]{1,0:T(8,128)} custom-call(bf16[12,192,384]{2,1,0:T(8,128)(2,1)} %bitcast.137), custom_call_target="tpu_custom_call" | custom-call | tf_op jit(solution)/shard_map/pallas_call | solution.py:705
  324.1 4.3 shard_map.165
  345.4 4.0 copy.89
  351.3 4.0 copy.90
  357.2 4.0 copy.91
  361.2 3.6 pad_maximum_fusion.1
  364.8 4.4 copy.95
  369.3 7.3 %copy.96 = bf16[2,2,2,4,192,576]{5,4,3,2,1,0:T(8,128)(2,1)} copy(bf16[2,2,2,4,192,576]{5,4,2,1,3,0:T(8,128)(2,1)} %bitcast.109) | data formatting | bytes 14155776 | tf_op jit(solution)/shard_map/transpose | solution.py:530
  383.2 4.0 copy.76
  389.1 3.9 copy.75
  400.0 3.9 concatenate.31
  403.9 3.9 copy.74
  407.8 3.9 pad_maximum_fusion
  411.7 4.4 copy.81
  416.1 7.2 %copy.82 = bf16[2,2,2,4,192,576]{5,4,3,2,1,0:T(8,128)(2,1)} copy(bf16[2,2,2,4,192,576]{5,4,1,2,3,0:T(8,128)(2,1)} %bitcast.110) | data formatting | bytes 14155776 | tf_op jit(solution)/shard_map/transpose | solution.py:530
  424.0 175.6 %shard_map.166 = (f32[192,576]{1,0:T(8,128)}, f32[192,576]{1,0:T(8,128)}, f32[8,576]{1,0:T(8,128)}) custom-call(bf16[32,192,576]{2,1,0:T(8,128)(2,1)} %bitcast.108, bf16[32,192,576]{2,1,0:T(8,128)(2,1)} %bitcast.107, f32[8,576]{1,0:T(8,128)} %concatenate.33.refs_2_), custom_call_target="tpu_custom_call" | custom-call | tf_op jit(solution)/shard_map/pallas_call | solution.py:547
  (136 shorter events, 82.8 us)
Async XLA Ops:
  7.2 4.2 copy-start.5
  7.2 58.0 %all-gather.8.cloned.1.call-start = ((), (), s32[]{:S(2)}) async-start(), calls=%async_computation.2 | async-start | bytes 5898240 | tf_op jit(solution)/shard_map/all_gather | solution.py:597
  11.3 2.5 copy-start.6
  11.3 58.3 %all-gather.6.cloned.1.call-start = ((), (), s32[]{:S(2)}) async-start(), calls=%async_computation.1 | async-start | bytes 5898240 | tf_op jit(solution)/shard_map/all_gather | solution.py:596
  13.7 60.3 %all-gather.4.cloned.1.call-start = ((), (), s32[]{:S(2)}) async-start(), calls=%async_computation | async-start | bytes 5898240 | tf_op jit(solution)/shard_map/all_gather | solution.py:595
  18.6 2.5 copy-start.27
  25.1 5.8 copy-start.21
  25.1 9.0 %copy-start = (bf16[2,576,576]{2,1,0:T(8,128)(2,1)S(1)}, bf16[2,576,576]{2,1,0:T(8,128)(2,1)}, u32[]{:S(2)}) copy-start(bf16[2,576,576]{2,1,0:T(8,128)(2,1)} %copy.97) | copy-start | bytes 3981316
  28.3 5.8 copy-start.3
  28.3 5.8 copy-start.4
  62.6 2.0 copy-start.22
  242.7 4.4 copy-start.20
  251.2 3.1 copy-start.1
  324.0 4.3 copy-start.17
  334.7 2.7 copy-start.7
  337.0 0.9 copy-start.10
  340.6 2.8 copy-start.9
  340.6 2.8 copy-start.14
  345.4 4.0 copy-start.13
  351.3 4.0 copy-start.12
  351.3 4.0 copy-start.18
  369.2 7.3 %copy-start.11 = (bf16[192,1536]{1,0:T(8,128)(2,1)S(1)}, bf16[192,1536]{1,0:T(8,128)(2,1)}, u32[]{:S(2)}) copy-start(bf16[192,1536]{1,0:T(8,128)(2,1)} %get-tuple-element.86) | copy-start | bytes 1769476
  369.3 7.3 %copy-start.19 = (bf16[192,576]{1,0:T(8,128)(2,1)S(1)}, bf16[192,576]{1,0:T(8,128)(2,1)}, u32[]{:S(2)}) copy-start(bf16[192,576]{1,0:T(8,128)(2,1)} %get-tuple-element.87) | copy-start | bytes 663556
  378.4 2.8 copy-start.8
  378.4 2.8 copy-start.16
  383.2 4.0 copy-start.15
  393.0 3.6 copy-start.2
  416.1 7.3 %copy-start.23 = (f32[1,576]{1,0:T(1,128)S(1)}, f32[1,576]{1,0:T(1,128)}, u32[]{:S(2)}) copy-start(f32[1,576]{1,0:T(1,128)} %get-tuple-element.98) | copy-start | bytes 6916
  416.1 7.3 %copy-start.24 = (f32[1,576]{1,0:T(1,128)S(1)}, f32[1,576]{1,0:T(1,128)}, u32[]{:S(2)}) copy-start(f32[1,576]{1,0:T(1,128)} %get-tuple-element.97) | copy-start | bytes 6916
  416.1 7.3 %copy-start.25 = (f32[1,576]{1,0:T(1,128)S(1)}, f32[1,576]{1,0:T(1,128)}, u32[]{:S(2)}) copy-start(f32[1,576]{1,0:T(1,128)} %get-tuple-element.96) | copy-start | bytes 6916
  416.1 7.3 %copy-start.26 = (f32[1,576]{1,0:T(1,128)S(1)}, f32[1,576]{1,0:T(1,128)}, u32[]{:S(2)}) copy-start(f32[1,576]{1,0:T(1,128)} %get-tuple-element.95) | copy-start | bytes 6916
Sparse Core Ops, SparseCore 0:
  11.4 15.9 all-gather.7
  29.0 14.4 all-gather.5
  45.0 14.4 all-gather.3

commit v3 on v2

--- a/solution.py
+++ b/solution.py
@@ -93,45 +93,79 @@
     return {"dp": lax.div(index, pair), "tensor": lax.rem(index, pair)}
 
 
-def greet(me, count, reach, step):
+def greet(me, count, reach, step, senders_pair, copies_pair):
     barrier = pltpu.get_barrier_semaphore()
-    pair = lax.axis_size("tensor")
-    for by in range(1, reach + 1):
-        sender = me + step * by
-
-        @pl.when((sender >= 0) & (sender < count))
+    core = lax.rem(me, 2)
+    far_sender = 0 if step < 0 else 1
+    waits = jnp.where(copies_pair, 1, 0)
+    for by in list(range(2, reach, 2)) + [reach]:
+        sender, target = me + step * by, me - step * by
+        hears = (sender >= 0) & (sender < count)
+        sends = (target >= 0) & (target < count)
+        if by == reach:
+            hears = hears & (core == far_sender)
+            sends = sends & (core == 1 - far_sender)
+
+        @pl.when(hears)
         def _():
             pl.semaphore_signal(
-                barrier, inc=1, device_id=mesh_id(sender, pair), device_id_type=MESH
+                barrier, inc=1, device_id=mesh_id(sender, 2), device_id_type=MESH
             )
 
-    copied_to = jnp.minimum(count - 1 - me if step < 0 else me, reach)
-
-    @pl.when(copied_to > 0)
+        waits = waits + jnp.where(sends, 1, 0)
+
+    @pl.when(senders_pair)
     def _():
-        pl.semaphore_wait(barrier, copied_to)
-
-
-def fetch_kernel(count, reach, own_ref, window_ref, send_sem, recv_sem):
-    pair = lax.axis_size("tensor")
-    me = lax.axis_index("dp") * pair + lax.axis_index("tensor")
-    greet(me, count, reach, -1)
+        pl.semaphore_signal(
+            barrier, inc=1, device_id=mesh_id(me + 1 - 2 * core, 2), device_id_type=MESH
+        )
+
+    @pl.when(waits > 0)
+    def _():
+        pl.semaphore_wait(barrier, waits)
+
+
+def fetch_kernel(count, reach, own_ref, window_ref, send_sem, recv_sem, pass_sem):
+    core = lax.axis_index("tensor")
+    me = lax.axis_index("dp") * 2 + core
+    sibling = me + 1 - 2 * core
+    greet(me, count, reach, -1, (core == 1) | (me > 0), (core == 0) | (me > 1))
 
     def send(by):
         return pltpu.make_async_remote_copy(
             src_ref=own_ref,
             dst_ref=window_ref.at[reach - by],
-            send_sem=send_sem.at[by - 1],
-            recv_sem=recv_sem.at[by - 1],
-            device_id=mesh_id(me + by, pair),
+            send_sem=send_sem.at[by],
+            recv_sem=recv_sem.at[by],
+            device_id=mesh_id(me + by, 2),
             device_id_type=MESH,
         )
 
-    for by in range(1, reach + 1):
+    def hand_over(by):
+        there = by + 1 - 2 * core
+        return pltpu.make_async_remote_copy(
+            src_ref=own_ref if by == 0 else window_ref.at[reach - by],
+            dst_ref=window_ref.at[reach - there],
+            send_sem=pass_sem.at[by],
+            recv_sem=recv_sem.at[there],
+            device_id=mesh_id(sibling, 2),
+            device_id_type=MESH,
+        )
+
+    even = list(range(2, reach, 2))
+    for by in even:
 
         @pl.when(me + by < count)
         def _():
             send(by).start()
+
+    @pl.when((core == 1) & (me + reach < count))
+    def _():
+        send(reach).start()
+
+    @pl.when(core == 0)
+    def _():
+        hand_over(0).start()
 
     window_ref[reach] = own_ref[...]
     for by in range(1, reach + 1):
@@ -140,49 +174,136 @@
         def _():
             window_ref[reach - by] = jnp.zeros(own_ref.shape, own_ref.dtype)
 
-    for by in range(1, reach + 1):
+    for by in even:
 
         @pl.when(me - by >= 0)
         def _():
             send(by).wait_recv()
+            hand_over(by).start()
+
+    for by in range(1, reach + 1, 2):
+
+        @pl.when(me - by >= 0)
+        def _():
+            send(by).wait_recv()
+
+    for by in even:
+
+        @pl.when(me - by >= 0)
+        def _():
+            hand_over(by).wait_send()
 
         @pl.when(me + by < count)
         def _():
             send(by).wait_send()
 
-
-def return_kernel(count, reach, grads_ref, sum_ref, held, send_sem, recv_sem):
-    pair = lax.axis_size("tensor")
-    me = lax.axis_index("dp") * pair + lax.axis_index("tensor")
-    greet(me, count, reach, 1)
+    @pl.when((core == 1) & (me + reach < count))
+    def _():
+        send(reach).wait_send()
+
+    @pl.when(core == 0)
+    def _():
+        hand_over(0).wait_send()
+
+
+def return_kernel(
+    count, reach, grads_ref, sum_ref, near, joined, held, send_sem, recv_sem, pass_sem, near_sem
+):
+    core = lax.axis_index("tensor")
+    me = lax.axis_index("dp") * 2 + core
+    sibling = me + 1 - 2 * core
+    greet(me, count, reach, 1, (core == 0) | (me > 1), (core == 1) | (me > 0))
+    even = list(range(2, reach, 2))
+
+    def hand_over(by):
+        slot = (by + 1) // 2 - core
+        return pltpu.make_async_remote_copy(
+            src_ref=grads_ref.at[reach - by],
+            dst_ref=near.at[slot],
+            send_sem=pass_sem.at[by],
+            recv_sem=near_sem.at[slot],
+            device_id=mesh_id(sibling, 2),
+            device_id_type=MESH,
+        )
+
+    def taken(slot):
+        return pltpu.make_async_remote_copy(
+            src_ref=grads_ref.at[0],
+            dst_ref=near.at[slot],
+            send_sem=pass_sem.at[0],
+            recv_sem=near_sem.at[slot],
+            device_id=mesh_id(sibling, 2),
+            device_id_type=MESH,
+        )
 
     def send(by):
         return pltpu.make_async_remote_copy(
-            src_ref=grads_ref.at[reach - by],
-            dst_ref=held.at[by - 1],
-            send_sem=send_sem.at[by - 1],
-            recv_sem=recv_sem.at[by - 1],
-            device_id=mesh_id(me - by, pair),
+            src_ref=grads_ref.at[0] if by == reach else joined.at[by // 2 - 1],
+            dst_ref=held.at[by // 2 - 1 + by % 2],
+            send_sem=send_sem.at[by],
+            recv_sem=recv_sem.at[by],
+            device_id=mesh_id(me - by, 2),
             device_id_type=MESH,
         )
 
-    for by in range(reach, 0, -1):
+    @pl.when((core == 0) & (me - reach >= 0))
+    def _():
+        send(reach).start()
+
+    for by in range(reach, 0, -2):
+        wanted = me - by >= 0
+        if by == reach:
+            wanted = wanted & (core == 1)
+
+        @pl.when(wanted)
+        def _():
+            hand_over(by).start()
+
+    for by in even[::-1]:
 
         @pl.when(me - by >= 0)
         def _():
+            taken(by // 2).wait_recv()
+            joined[by // 2 - 1] = (
+                grads_ref[reach - by].astype(jnp.float32) + near[by // 2].astype(jnp.float32)
+            ).astype(jnp.bfloat16)
             send(by).start()
 
     sum_ref[...] = grads_ref[reach].astype(jnp.float32)
-    for by in range(1, reach + 1):
-
-        @pl.when(me + by < count)
+
+    @pl.when(core == 0)
+    def _():
+        taken(0).wait_recv()
+        sum_ref[...] += near[0].astype(jnp.float32)
+
+    for by in even + [reach]:
+        comes = me + by < count
+        if by == reach:
+            comes = comes & (core == 1)
+
+        @pl.when(comes)
         def _():
             send(by).wait_recv()
-            sum_ref[...] += held[by - 1].astype(jnp.float32)
+            sum_ref[...] += held[by // 2 - 1 + by % 2].astype(jnp.float32)
+
+    for by in even:
 
         @pl.when(me - by >= 0)
         def _():
             send(by).wait_send()
+
+    @pl.when((core == 0) & (me - reach >= 0))
+    def _():
+        send(reach).wait_send()
+
+    for by in range(reach, 0, -2):
+        wanted = me - by >= 0
+        if by == reach:
+            wanted = wanted & (core == 1)
+
+        @pl.when(wanted)
+        def _():
+            hand_over(by).wait_send()
 
 
 def allowed_pairs(chunk, rows, low_ref, high_ref):
@@ -509,6 +630,43 @@
     return 1, 1, count
 
 
+def block_order(order, extent, blocks):
+    there = []
+    for block in range(blocks):
+        at, left = {}, block
+        for axis in "xyzt":
+            at[axis], left = left % extent[axis], left // extent[axis]
+        slot = 0
+        for axis in order:
+            slot = slot * extent[axis] + at[axis]
+        there.append(slot)
+    return there
+
+
+def weight_kernel(slots, pair, gqkv_ref, a_ref, go_ref, o_ref, ggate_ref, gup_ref, m_ref, hidden_ref, gy_ref, out_ref, attn_ref):
+    bf16 = jnp.bfloat16
+    blocks, rows, _ = out_ref.shape
+    piece = rows // 4
+    chips = blocks // pair
+    inward = cols_by_cols(gqkv_ref[...], a_ref[...]).astype(bf16)
+    starts = [head * TILE for head in range(H + KV)]
+    starts += [(H + head) * TILE + HD for head in range(KV)]
+    for place, start in enumerate(starts):
+        attn_ref[place * HD : (place + 1) * HD, :] = inward[start : start + HD]
+    attn_ref[len(starts) * HD :, :] = cols_by_cols(go_ref[...], o_ref[...]).astype(bf16)
+    for block in range(blocks):
+        core, chip = block // chips, block % chips
+        first = (chip * pair + core) * piece
+        out_ref[slots[block], 0:piece, :] = attn_ref[first : first + piece, :]
+    grads = ((ggate_ref, m_ref), (gup_ref, m_ref), (hidden_ref, gy_ref))
+    for slot, (left, right) in enumerate(grads):
+        product = cols_by_cols(left[...], right[...]).astype(bf16)
+        for block in range(blocks):
+            out_ref[slots[block], (slot + 1) * piece : (slot + 2) * piece, :] = product[
+                block * piece : (block + 1) * piece
+            ]
+
+
 def sum_grads(layer_parts, gains):
     bf16 = jnp.bfloat16
     pair = lax.axis_size("tensor")
@@ -518,17 +676,39 @@
     orders = ["txyz" if part % 2 == 0 else "tyxz" for part in range(len(layer_parts))]
     chips = across * up * deep
     stacked = []
-    for order, (attn, *ffn) in zip(orders, layer_parts):
-        pieces = attn.shape[0] // (chips * pair)
-        split = [jnp.transpose(attn.reshape(chips, pair, pieces, width), (1, 0, 2, 3))]
-        split += [part.reshape(pair, chips, pieces, width) for part in ffn]
-        whole = jnp.stack(split, axis=2).reshape(
-            pair, deep, up, across, len(split) * pieces, width
-        )
+    for order, operands in zip(orders, layer_parts):
+        gqkv, a, go, o, ggate, gup, m, hidden, gy = operands
+        blocks = pair * chips
+        piece = hidden.shape[1] // blocks
+        if piece % 16 == 0:
+            slots = block_order(order, extent, blocks)
+            stacked.append(
+                call(
+                    functools.partial(weight_kernel, tuple(slots), pair),
+                    jax.ShapeDtypeStruct((blocks, 4 * piece, width), bf16),
+                    [pltpu.VMEM((hidden.shape[1], width), bf16)],
+                )(*operands)
+            )
+            continue
+        ffn = [
+            cols_by_cols(left, right).astype(bf16)
+            for left, right in ((ggate, m), (gup, m), (hidden, gy))
+        ]
+        g_in = cols_by_cols(gqkv, a).reshape(H + KV, 2, HD, width)
+        attn = jnp.concatenate(
+            [
+                g_in[:H, 0].reshape(H * HD, width),
+                g_in[H:, 0].reshape(KV * HD, width),
+                g_in[H:, 1].reshape(KV * HD, width),
+                cols_by_cols(go, o),
+            ],
+            axis=0,
+        ).astype(bf16)
+        split = [jnp.transpose(attn.reshape(chips, pair, piece, width), (1, 0, 2, 3))]
+        split += [part.reshape(pair, chips, piece, width) for part in ffn]
+        whole = jnp.stack(split, axis=2).reshape(pair, deep, up, across, 4 * piece, width)
         turn = (0, 3, 2, 1, 4, 5) if order == "txyz" else (0, 2, 3, 1, 4, 5)
-        stacked.append(
-            jnp.transpose(whole, turn).reshape(pair * chips, len(split) * pieces, width)
-        )
+        stacked.append(jnp.transpose(whole, turn).reshape(blocks, 4 * piece, width))
     rows = stacked[0].shape[1]
     stages = 4
     kept, held = [], []
@@ -569,7 +749,8 @@
     layers = w_attn.shape[0]
     count = lax.axis_size("dp") * lax.axis_size("tensor")
     qkv_rows = (H + 2 * KV) * HD
-    reach = min((L_MAX + own - 2) // own, count - 1)
+    reach = (L_MAX + own - 2) // own
+    reach += 1 - reach % 2
     window_rows = (reach + 1) * own
     chunk_rows = 2 * own if (reach + 1) % 2 == 0 else own
     tiles = (H + KV) * TILE
@@ -624,7 +805,7 @@
         window = call(
             functools.partial(fetch_kernel, count, reach),
             shape((reach + 1, own, KV * TILE), bf16),
-            [pltpu.SemaphoreType.DMA((reach,)), pltpu.SemaphoreType.DMA((reach,))],
+            [pltpu.SemaphoreType.DMA((reach + 1,)) for _ in range(3)],
             collective_id=0,
             has_side_effects=True,
         )(kv_own).reshape(window_rows, KV * TILE)
@@ -706,10 +887,11 @@
             functools.partial(return_kernel, count, reach),
             shape((own, KV * TILE), f32),
             [
-                pltpu.VMEM((reach, own, KV * TILE), bf16),
-                pltpu.SemaphoreType.DMA((reach,)),
-                pltpu.SemaphoreType.DMA((reach,)),
-            ],
+                pltpu.VMEM((reach // 2 + 1, own, KV * TILE), bf16),
+                pltpu.VMEM((reach // 2, own, KV * TILE), bf16),
+                pltpu.VMEM((reach // 2 + 1, own, KV * TILE), bf16),
+            ]
+            + [pltpu.SemaphoreType.DMA((reach + 1,)) for _ in range(4)],
             collective_id=1,
             has_side_effects=True,
         )(gwin.reshape(reach + 1, own, KV * TILE))
@@ -723,22 +905,7 @@
         )(gq, gkv, cos_q, cos_kv, sin_all, w_in[layer], x_in, attn_gain[layer][None], gmid)
         gains.append((gain_a, gain_m))
 
-        ffn = [
-            cols_by_cols(left, right).astype(bf16)
-            for left, right in ((ggate, normed_m), (gup, normed_m), (hidden, gy))
-        ]
-        g_out = cols_by_cols(go, heads)
-        g_in = cols_by_cols(gqkv, normed).reshape(H + KV, 2, HD, width)
-        attn_part = jnp.concatenate(
-            [
-                g_in[:H, 0].reshape(H * HD, width),
-                g_in[H:, 0].reshape(KV * HD, width),
-                g_in[H:, 1].reshape(KV * HD, width),
-                g_out,
-            ],
-            axis=0,
-        ).astype(bf16)
-        parts.append([attn_part, *ffn])
+        parts.append([gqkv, normed, go, heads, ggate, gup, normed_m, hidden, gy])
     rows = [row for pair in gains[::-1] for row in pair]
     rows.append(jnp.zeros((-len(rows) % 8, width), f32))
     sums, gain_sums = sum_grads(parts[::-1], jnp.concatenate(rows, axis=0))

time: 624 us -> 459 us (0.74)
  local copies, waits for them, and re-layouts: 122 us -> 47.9 us
  Pallas kernels: 441 us -> 380 us
  matrix products: 16.7 us -> 0 us
  other arithmetic: 19.3 us -> 11 us
    pallas_call x2, Pallas kernels: 66.3 us -> 37.5 us  [body(): call(functools.partial(fetch_kernel, count, reach), shape((reach + 1, own...]
    pallas_call x2, Pallas kernels: 88.7 us -> 60.6 us  [body(): call(functools.partial(return_kernel, count, reach), shape((own, KV * TIL...]
    convert_element_type x6 -> x0, local copies, waits for them, and re-layouts: 22.7 us -> none  [body(): cols_by_cols(left, right).astype(bf16)]
    pallas_call x1, Pallas kernels: 176 us -> 155 us  [sum_grads(): call(functools.partial(sum_kernel, (pair, across, up, deep), tuple(orders...]
    another operation x10 -> x0, local copies, waits for them, and re-layouts: 17.7 us -> none  [the longest x2 8.85 us: sum_grads(): jnp.stack(split, axis=2)]
    dot_general x10 -> x0, matrix products: 16.7 us -> none  [cols_by_cols(): lax.dot_general(left, right, (((0,), (0,)), ((), ())), preferred_element_...]
    pallas_call x0 -> x2, Pallas kernels: none -> 16.6 us  [sum_grads(): call(functools.partial(weight_kernel, tuple(slots), pair), jax.ShapeDtype...]
    transpose x2 -> x0, local copies, waits for them, and re-layouts: 14.5 us -> none  [sum_grads(): jnp.transpose(whole, turn).reshape(pair * chips, len(split) * pieces, width)]
  transfers between devices with their start and end apart: 3 -> 3, of which waited for: 0 -> 0; matrix products, arithmetic and copies ran while one was open for 6% -> 8% of each run, Pallas kernels for 4% -> 4%
where the time goes in v3:
time: 459 us; the launch traced here: 453 us
  Pallas kernels  380 us (83%)
  local copies, waits for them, and re-layouts  47.9 us (10%)
  between operations  14.2 us (3%)
  other arithmetic  11 us (2%)
    pallas_call x1, Pallas kernels, sum_grads(): call(functools.partial(sum_kernel, (pair, across, up, deep), tuple(orders...  155 us
    pallas_call x2, Pallas kernels, body(): call(functools.partial(return_kernel, count, reach), shape((own, KV * TIL...  60.6 us
    pallas_call x2, Pallas kernels, body(): call(functools.partial(attend_kernel, chunk_rows), (shape((own, width), f...  41.4 us
    pallas_call x2, Pallas kernels, body(): call(functools.partial(attend_back_kernel, chunk_rows), (shape((KV, GROUP...  38.8 us
    pallas_call x2, Pallas kernels, body(): call(functools.partial(fetch_kernel, count, reach), shape((reach + 1, own...  37.5 us
    pallas_call x2, Pallas kernels, sum_grads(): call(functools.partial(weight_kernel, tuple(slots), pair), jax.ShapeDtype...  16.6 us
    unnamed x32, local copies, waits for them, and re-layouts  13.9 us
    pallas_call x2, Pallas kernels, body(): call(mlp_back_kernel, (shape((own, width), bf16), shape((own, hidden_rows...  13.4 us
  transfers between devices with their start and end apart: 3, of which 0 were waited for; matrix products, arithmetic and copies ran while one was open for 8% of the time, Pallas kernels for 4%

profile of v3, /device:TPU:0, one launch (start us, length us, event | category | flops | bytes accessed | tf_op | source)
XLA Modules:
  0.0 453.1 jit_solution(13497575147973373845)
XLA Ops:
  7.2 4.1 copy.40
  11.4 2.3 copy.39
  13.8 2.3 copy.38
  16.1 2.6 fusion.9
  18.7 2.6 fusion.10
  23.7 1.6 copy.45
  25.3 2.2 copy.46
  28.5 1.8 convert_element_type.16.x_ref
  32.7 1.5 fusion.4
  34.7 2.4 fusion.8
  37.1 4.1 shard_map.152
  41.2 13.9 %shard_map.153 = bf16[12,192,384]{2,1,0:T(8,128)(2,1)} custom-call(bf16[192,384]{1,0:T(8,128)(2,1)} %get-tuple-element.56.own_ref), custom_call_target="tpu_custom_call" | custom-call | tf_op jit(solution)/shard_map/pallas_call | solution.py:805
  56.4 2.0 fusion.3
  59.0 4.4 slice_bitcast_fusion
  63.5 4.4 slice_bitcast_fusion.1
  67.8 4.4 slice_bitcast_fusion.2
  72.2 20.7 %shard_map.154 = (f32[192,576]{1,0:T(8,128)}, f32[192,576]{1,0:T(8,128)}, bf16[192,576]{1,0:T(8,128)(2,1)}, f32[192,1536]{1,0:T(8,128)}, f32[192,1536]{1,0:T(8,1...) custom-call(bf16[3,576,128]{2,1,0:T(8,128)(2,1)} %get-tuple-element.55.q_ref, ...), custom_call_target="tpu_custom_call" | custom-call | tf_op jit(solution)/shard_map/pallas_call | solution.py:813
  92.8 3.7 shard_map.155
  96.5 23.6 %shard_map.156 = bf16[12,192,384]{2,1,0:T(8,128)(2,1)} custom-call(bf16[192,384]{1,0:T(8,128)(2,1)} %get-tuple-element.59.own_ref), custom_call_target="tpu_custom_call" | custom-call | tf_op jit(solution)/shard_map/pallas_call | solution.py:805
  120.1 20.7 %shard_map.157 = (f32[192,576]{1,0:T(8,128)}, f32[192,576]{1,0:T(8,128)}, bf16[192,576]{1,0:T(8,128)(2,1)}, f32[192,1536]{1,0:T(8,128)}, f32[192,1536]{1,0:T(8,1...) custom-call(bf16[3,576,128]{2,1,0:T(8,128)(2,1)} %get-tuple-element.58.q_ref, ...), custom_call_target="tpu_custom_call" | custom-call | tf_op jit(solution)/shard_map/pallas_call | solution.py:813
  142.0 6.7 %shard_map.158 = (bf16[192,576]{1,0:T(8,128)(2,1)}, bf16[192,1536]{1,0:T(8,128)(2,1)}, bf16[192,1536]{1,0:T(8,128)(2,1)}, f32[192,576]{1,0:T(8,128)}, bf16[192,576]{1,0:T(8,128)(2,1)}, /*index=5*/f32[1,576]{1,0:T(1,128)}) custom-call(bf16[192,576]{1,0:T(8,128)(2,1)} %gx_ref.1, f32[192,576]{1,0:T(8,128)} %get-tuple-element.61.mid_ref, ...), custom_call_target="tpu_custom_call" | custom-call | tf_op jit(solution)/shard_map/pallas_call | solution.py:851
  148.7 19.4 %shard_map.159 = (f32[3,576,128]{2,1,0:T(8,128)}, bf16[2304,384]{1,0:T(8,128)(2,1)}) custom-call(bf16[192,576]{1,0:T(8,128)(2,1)} %get-tuple-element.64.go_ref, bf16[9,128,576]{2,1,0:T(8,128)(2,1)} %get-tuple-element.114.wo_ref, bf16[3,576,128]{2,1,0:T(8,128)(2,1)} %get-tuple-element.58.q_ref, bf16[2304,384]{1,0:T(8,128)(2,1)} %bitcast.62, ...), custom_call_target="tpu_custom_call" | custom-call | tf_op jit(solution)/shard_map/pallas_call | solution.py:874
  168.1 30.6 %shard_map.160.gkv_ref = f32[192,384]{1,0:T(8,128)} custom-call(bf16[12,192,384]{2,1,0:T(8,128)(2,1)} %bitcast.68), custom_call_target="tpu_custom_call" | custom-call | tf_op jit(solution)/shard_map/pallas_call | solution.py:886
  198.8 4.3 shard_map.161
  203.1 6.7 %shard_map.162 = (bf16[192,576]{1,0:T(8,128)(2,1)}, bf16[192,1536]{1,0:T(8,128)(2,1)}, bf16[192,1536]{1,0:T(8,128)(2,1)}, f32[192,576]{1,0:T(8,128)}, bf16[192,576]{1,0:T(8,128)(2,1)}, /*index=5*/f32[1,576]{1,0:T(1,128)}) custom-call(f32[192,576]{1,0:T(8,128)} %get-tuple-element.70.gx_ref, f32[192,576]{1,0:T(8,128)} %get-tuple-element.71.mid_ref, ...), custom_call_target="tpu_custom_call" | custom-call | tf_op jit(solution)/shard_map/pallas_call | solution.py:851
  209.8 19.4 %shard_map.163 = (f32[3,576,128]{2,1,0:T(8,128)}, bf16[2304,384]{1,0:T(8,128)(2,1)}) custom-call(bf16[192,576]{1,0:T(8,128)(2,1)} %get-tuple-element.74.go_ref, bf16[9,128,576]{2,1,0:T(8,128)(2,1)} %get-tuple-element.115.wo_ref, bf16[3,576,128]{2,1,0:T(8,128)(2,1)} %get-tuple-element.55.q_ref, bf16[2304,384]{1,0:T(8,128)(2,1)} %bitcast.60, ...), custom_call_target="tpu_custom_call" | custom-call | tf_op jit(solution)/shard_map/pallas_call | solution.py:874
  229.1 30.1 %shard_map.164.gkv_ref = f32[192,384]{1,0:T(8,128)} custom-call(bf16[12,192,384]{2,1,0:T(8,128)(2,1)} %bitcast.67), custom_call_target="tpu_custom_call" | custom-call | tf_op jit(solution)/shard_map/pallas_call | solution.py:886
  261.8 4.3 shard_map.165
  266.1 1.3 concatenate.23.refs_2_
  267.4 8.3 %shard_map.167.refs_1_ = bf16[32,192,576]{2,1,0:T(8,128)(2,1)} custom-call(bf16[192,1536]{1,0:T(8,128)(2,1)} %get-tuple-element.88.gqkv_ref, bf16[192,576]{1,0:T(8,128)(2,1)} %get-tuple-element.89.a_ref, bf16[192,576]{1,0:T(8,128)(2,1)} %get-tuple-element.64.go_ref, bf16[192,576]{1,0:T(8,128)(2,1)} %copy.44.o_ref, ...), custom_call_target="tpu_custom_call" | custom-call | tf_op jit(solution)/shard_map/pallas_call | solution.py:686
  275.7 8.3 %shard_map.166.refs_0_ = bf16[32,192,576]{2,1,0:T(8,128)(2,1)} custom-call(bf16[192,1536]{1,0:T(8,128)(2,1)} %get-tuple-element.81.gqkv_ref, bf16[192,576]{1,0:T(8,128)(2,1)} %get-tuple-element.82.a_ref, bf16[192,576]{1,0:T(8,128)(2,1)} %get-tuple-element.74.go_ref, bf16[192,576]{1,0:T(8,128)(2,1)} %copy.42.o_ref, ...), custom_call_target="tpu_custom_call" | custom-call | tf_op jit(solution)/shard_map/pallas_call | solution.py:686
  284.0 155.2 %shard_map.168 = (f32[192,576]{1,0:T(8,128)}, f32[192,576]{1,0:T(8,128)}, f32[8,576]{1,0:T(8,128)}) custom-call(bf16[32,192,576]{2,1,0:T(8,128)(2,1)} %shard_map.166.refs_0_, bf16[32,192,576]{2,1,0:T(8,128)(2,1)} %shard_map.167.refs_1_, f32[8,576]{1,0:T(8,128)} %concatenate.23.refs_2_), custom_call_target="tpu_custom_call" | custom-call | tf_op jit(solution)/shard_map/pallas_call | solution.py:727
  (70 shorter events, 19.3 us)
Async XLA Ops:
  7.2 4.2 copy-start.4
  7.2 51.9 %all-gather.8.cloned.1.call-start = ((), (), s32[]{:S(2)}) async-start(), calls=%async_computation.2 | async-start | bytes 5898240 | tf_op jit(solution)/shard_map/all_gather | solution.py:778
  11.3 2.4 copy-start.5
  11.3 52.2 %all-gather.6.cloned.1.call-start = ((), (), s32[]{:S(2)}) async-start(), calls=%async_computation.1 | async-start | bytes 5898240 | tf_op jit(solution)/shard_map/all_gather | solution.py:777
  13.7 54.1 %all-gather.4.cloned.1.call-start = ((), (), s32[]{:S(2)}) async-start(), calls=%async_computation | async-start | bytes 5898240 | tf_op jit(solution)/shard_map/all_gather | solution.py:776
  18.7 2.6 copy-start.11
  25.3 5.8 %copy-start.6 = (f32[2,576]{1,0:T(2,128)S(1)}, f32[2,576]{1,0:T(2,128)}, u32[]{:S(2)}) copy-start(f32[2,576]{1,0:T(2,128)} %param.11) | copy-start | bytes 13828
  25.3 9.0 %copy-start = (bf16[2,576,576]{2,1,0:T(8,128)(2,1)S(1)}, bf16[2,576,576]{2,1,0:T(8,128)(2,1)}, u32[]{:S(2)}) copy-start(bf16[2,576,576]{2,1,0:T(8,128)(2,1)} %copy.45) | copy-start | bytes 3981316
  28.5 5.8 %copy-start.2 = (bf16[2,192,576]{2,1,0:T(8,128)(2,1)S(1)}, bf16[2,192,576]{2,1,0:T(8,128)(2,1)}, u32[]{:S(2)}) copy-start(bf16[2,192,576]{2,1,0:T(8,128)(2,1)} %copy.46) | copy-start | bytes 1327108
  28.5 5.8 %copy-start.3 = (bf16[2,192,576]{2,1,0:T(8,128)(2,1)S(1)}, bf16[2,192,576]{2,1,0:T(8,128)(2,1)}, u32[]{:S(2)}) copy-start(bf16[2,192,576]{2,1,0:T(8,128)(2,1)} %copy.47) | copy-start | bytes 1327108
  56.4 2.0 copy-start.7
  168.1 30.6 %copy-start.1 = (f32[3,576,128]{2,1,0:T(8,128)S(1)}, f32[3,576,128]{2,1,0:T(8,128)}, u32[]{:S(2)}) copy-start(f32[3,576,128]{2,1,0:T(8,128)} %get-tuple-element.75.o_ref) | copy-start | bytes 2654212
  261.8 4.3 copy-start.8
  261.8 4.3 copy-start.9
  261.8 4.3 copy-start.10
Sparse Core Ops, SparseCore 0:
  11.4 15.9 all-gather.7
  29.0 14.4 all-gather.5
  45.0 14.4 all-gather.3

commit v4 on v3

--- a/solution.py
+++ b/solution.py
@@ -63,23 +63,59 @@
     )
 
 
-def call(kernel, out_shape, scratch=(), **params):
+def call(kernel, out_shape, scratch=(), specs=None, **params):
+    given = {}
+    if specs is not None:
+        given = {"grid": (1,), "in_specs": specs, "out_specs": tuple(whole_spec() for _ in out_shape)}
     return pl.pallas_call(
         kernel,
         out_shape=out_shape,
+        **given,
         scratch_shapes=list(scratch),
         compiler_params=pltpu.CompilerParams(vmem_limit_bytes=VMEM_LIMIT, **params),
     )
 
 
-def project_kernel(x_ref, gain_ref, w_ref, cq_ref, ckv_ref, sn_ref, q_ref, kv_ref, a_ref):
+def whole_spec():
+    return pl.BlockSpec(memory_space=pltpu.VMEM)
+
+
+def attn_spec(w_attn, layer):
+    return pl.BlockSpec((None,) + w_attn.shape[1:], lambda step: (layer, 0, 0))
+
+
+def ffn_spec(weights, layer):
+    pair, _, rows, width = weights.shape
+    return pl.BlockSpec((pair, None, rows, width), lambda step: (0, layer, 0, 0))
+
+
+def joined_rows(ref):
+    value = ref[...]
+    return value.reshape(value.shape[0] * value.shape[1], value.shape[2])
+
+
+def spread_rows(wide_ref, w_ref):
+    for head in range(H + KV):
+        start = head * TILE
+        wide_ref[start : start + HD, :] = w_ref[head * HD : (head + 1) * HD, :]
+        if head < H:
+            wide_ref[start + HD : start + TILE, :] = jnp.zeros(
+                (HD, wide_ref.shape[1]), wide_ref.dtype
+            )
+        else:
+            value = (head + KV) * HD
+            wide_ref[start + HD : start + TILE, :] = w_ref[value : value + HD, :]
+
+
+def project_kernel(x_ref, gain_ref, w_ref, cq_ref, ckv_ref, sn_ref, q_ref, kv_ref, a_ref, wide_ref):
     own = x_ref.shape[0]
+    spread_rows(wide_ref, w_ref)
     ratio, _ = rms_parts(x_ref[...])
     normed = (ratio * gain_ref[...]).astype(jnp.bfloat16)
     a_ref[...] = normed
     sines = sn_ref[...]
     for head in range(H + KV):
-        lin = rows_by_rows(normed, w_ref[head * TILE : (head + 1) * TILE, :])
+        lin = rows_by_rows(normed, wide_ref[head * TILE : (head + 1) * TILE, :])
         cosines = cq_ref[...] if head < H else ckv_ref[...]
         turned = (lin * cosines + swap_halves(lin) * sines).astype(jnp.bfloat16)
         if head < H:
@@ -369,13 +405,13 @@
     ratio, _ = rms_parts(middle)
     normed = (ratio * gain_ref[...]).astype(jnp.bfloat16)
     m_ref[...] = normed
-    gate = rows_by_rows(normed, wg_ref[...])
-    up = rows_by_rows(normed, wu_ref[...])
+    gate = rows_by_rows(normed, joined_rows(wg_ref))
+    up = rows_by_rows(normed, joined_rows(wu_ref))
     gate_ref[...] = gate
     up_ref[...] = up
     hidden = (gate * jax.nn.sigmoid(gate) * up).astype(jnp.bfloat16)
     hidden_ref[...] = hidden
-    x_out_ref[...] = middle + plain_dot(hidden, wd_ref[...])
+    x_out_ref[...] = middle + plain_dot(hidden, joined_rows(wd_ref))
 
 
 def mlp_back_kernel(
@@ -397,14 +433,14 @@
     gx = gx_ref[...].astype(jnp.float32)
     gy = gx.astype(jnp.bfloat16)
     gy_ref[...] = gy
-    gh = rows_by_rows(gy, wd_ref[...])
+    gh = rows_by_rows(gy, joined_rows(wd_ref))
     gate = gate_ref[...]
     sig = jax.nn.sigmoid(gate)
     ggate = (gh * up_ref[...] * sig * (1.0 + gate * (1.0 - sig))).astype(jnp.bfloat16)
     gup = (gh * gate * sig).astype(jnp.bfloat16)
     ggate_ref[...] = ggate
     gup_ref[...] = gup
-    gm = plain_dot(ggate, wg_ref[...]) + plain_dot(gup, wu_ref[...])
+    gm = plain_dot(ggate, joined_rows(wg_ref)) + plain_dot(gup, joined_rows(wu_ref))
     ratio, inverse = rms_parts(mid_ref[...])
     back, ggain = norm_back(gm, ratio, inverse, gain_ref[...])
     ggain_ref[...] = ggain
@@ -468,9 +504,10 @@
 
 
 def project_back_kernel(
-    gq_ref, gkv_ref, cq_ref, ckv_ref, sn_ref, w_ref, x_ref, gain_ref, gmid_ref, gqkv_ref, gx_ref, ggain_ref
+    gq_ref, gkv_ref, cq_ref, ckv_ref, sn_ref, w_ref, x_ref, gain_ref, gmid_ref, gqkv_ref, gx_ref, ggain_ref, wide_ref
 ):
     own = x_ref.shape[0]
+    spread_rows(wide_ref, w_ref)
     sines = -sn_ref[...]
     for head in range(H + KV):
         if head < H:
@@ -482,7 +519,7 @@
             cosines = ckv_ref[...]
         turned = (lin * cosines + swap_halves(lin) * sines).astype(jnp.bfloat16)
         gqkv_ref[:, head * TILE : (head + 1) * TILE] = turned
-    grad_normed = plain_dot(gqkv_ref[...], w_ref[...])
+    grad_normed = plain_dot(gqkv_ref[...], wide_ref[...])
     ratio, inverse = rms_parts(x_ref[...])
     back, ggain = norm_back(grad_normed, ratio, inverse, gain_ref[...])
     ggain_ref[...] = ggain
@@ -603,17 +640,28 @@
             value += gain_held[stage][other]
         gain_sum[stage] = value
 
-    for part in range(parts):
-        start(part, 0)
+    def start_group(group):
+        for part in range(2 * group, 2 * group + 2):
+            start(part, 0)
+
+    groups = parts // 2
+    start_group(0)
     start_gain(0)
-    for stage in range(stages):
-        for part in range(parts):
-            finish(part, stage)
-            if stage < stages - 1:
-                start(part, stage + 1)
-        finish_gain(stage)
-        if stage < stages - 1:
-            start_gain(stage + 1)
+    for step in range(stages + groups - 1):
+        for group in range(groups):
+            stage = step - group
+            if not 0 <= stage < stages:
+                continue
+            for part in range(2 * group, 2 * group + 2):
+                finish(part, stage)
+                if stage < stages - 1:
+                    start(part, stage + 1)
+            if stage == 0 and group < groups - 1:
+                start_group(group + 1)
+        if step < stages:
+            finish_gain(step)
+            if step < stages - 1:
+                start_gain(step + 1)
     gain_out[...] = gain_sum[stages - 1]
     for stage in range(stages):
         for part in range(parts):
@@ -643,10 +691,10 @@
     return there
 
 
-def weight_kernel(slots, pair, gqkv_ref, a_ref, go_ref, o_ref, ggate_ref, gup_ref, m_ref, hidden_ref, gy_ref, out_ref, attn_ref):
+def weight_kernel(slots, pair, gqkv_ref, a_ref, go_ref, o_ref, ggate_ref, gup_ref, m_ref, hidden_ref, gy_ref, out_ref, late_ref, attn_ref):
     bf16 = jnp.bfloat16
     blocks, rows, _ = out_ref.shape
-    piece = rows // 4
+    piece = rows // 2
     chips = blocks // pair
     inward = cols_by_cols(gqkv_ref[...], a_ref[...]).astype(bf16)
     starts = [head * TILE for head in range(H + KV)]
@@ -662,7 +710,8 @@
     for slot, (left, right) in enumerate(grads):
         product = cols_by_cols(left[...], right[...]).astype(bf16)
         for block in range(blocks):
-            out_ref[slots[block], (slot + 1) * piece : (slot + 2) * piece, :] = product[
+            where, half = (out_ref, 1) if slot == 0 else (late_ref, slot - 1)
+            where[slots[block], half * piece : (half + 1) * piece, :] = product[
                 block * piece : (block + 1) * piece
             ]
 
@@ -685,7 +734,7 @@
             stacked.append(
                 call(
                     functools.partial(weight_kernel, tuple(slots), pair),
-                    jax.ShapeDtypeStruct((blocks, 4 * piece, width), bf16),
+                    (jax.ShapeDtypeStruct((blocks, 2 * piece, width), bf16),) * 2,
                     [pltpu.VMEM((hidden.shape[1], width), bf16)],
                 )(*operands)
             )
@@ -708,7 +757,12 @@
         split += [part.reshape(pair, chips, piece, width) for part in ffn]
         whole = jnp.stack(split, axis=2).reshape(pair, deep, up, across, 4 * piece, width)
         turn = (0, 3, 2, 1, 4, 5) if order == "txyz" else (0, 2, 3, 1, 4, 5)
-        stacked.append(jnp.transpose(whole, turn).reshape(blocks, 4 * piece, width))
+        stacked.append(
+            jnp.split(jnp.transpose(whole, turn).reshape(blocks, 4 * piece, width), 2, axis=1)
+        )
+    layers = len(stacked)
+    stacked = [halves[half] for half in range(2) for halves in stacked]
+    orders = orders * 2
     rows = stacked[0].shape[1]
     stages = 4
     kept, held = [], []
@@ -741,7 +795,8 @@
         collective_id=2,
         has_side_effects=True,
     )(*stacked, gains)
-    return [jnp.split(value, 4, axis=0) for value in sums], gain_sums
+    halves = [jnp.split(value, 2, axis=0) for value in sums]
+    return [halves[layer] + halves[layers + layer] for layer in range(layers)], gain_sums
 
 
 def body(tokens, w_attn, attn_gain, w_gate, w_up, w_down, mlp_gain, seq_lengths, cotangent):
@@ -773,19 +828,9 @@
     cos_kv = jnp.concatenate([cosines, cosines, ones], axis=1)
     sin_all = jnp.concatenate([-sines, sines, zeros], axis=1)
 
-    gate_all = lax.all_gather(w_gate, "tensor", axis=1, tiled=True)
-    up_all = lax.all_gather(w_up, "tensor", axis=1, tiled=True)
-    down_all = lax.all_gather(w_down, "tensor", axis=1, tiled=True)
-    q_rows = w_attn[:, : H * HD].reshape(layers, H, HD, width)
-    k_rows = w_attn[:, H * HD : (H + KV) * HD].reshape(layers, KV, HD, width)
-    v_rows = w_attn[:, (H + KV) * HD : qkv_rows].reshape(layers, KV, HD, width)
-    w_in = jnp.concatenate(
-        [
-            jnp.pad(q_rows, ((0, 0), (0, 0), (0, HD), (0, 0))),
-            jnp.concatenate([k_rows, v_rows], axis=2),
-        ],
-        axis=1,
-    ).reshape(layers, tiles, width)
+    gate_all = lax.all_gather(w_gate, "tensor", axis=0)
+    up_all = lax.all_gather(w_up, "tensor", axis=0)
+    down_all = lax.all_gather(w_down, "tensor", axis=0)
     w_out = jnp.pad(
         jnp.swapaxes(w_attn[:, qkv_rows:], 1, 2).reshape(layers, H, HD, width),
         ((0, 0), (0, 0), (HD, 0), (0, 0)),
@@ -801,7 +846,9 @@
                 shape((own, KV * TILE), bf16),
                 shape((own, width), bf16),
             ),
-        )(stream, attn_gain[layer][None], w_in[layer], cos_q, cos_kv, sin_all)
+            [pltpu.VMEM((tiles, width), bf16)],
+            [whole_spec()] * 2 + [attn_spec(w_attn, layer)] + [whole_spec()] * 3,
+        )(stream, attn_gain[layer][None], w_attn, cos_q, cos_kv, sin_all)
         window = call(
             functools.partial(fetch_kernel, count, reach),
             shape((reach + 1, own, KV * TILE), bf16),
@@ -809,7 +856,7 @@
             collective_id=0,
             has_side_effects=True,
         )(kv_own).reshape(window_rows, KV * TILE)
-        hidden_rows = gate_all.shape[1]
+        hidden_rows = gate_all.shape[0] * gate_all.shape[2]
         x_out, middle, normed_m, gate, up, hidden, mixed, lse = call(
             functools.partial(attend_kernel, chunk_rows),
             (
@@ -827,6 +874,7 @@
                 pltpu.VMEM((KV, 1, GROUPS * own), f32),
                 pltpu.VMEM((KV, 1, GROUPS * own), f32),
             ],
+            [whole_spec()] * 7 + [ffn_spec(gate_all, layer)] * 3,
         )(
             queries,
             window,
@@ -835,9 +883,9 @@
             stream,
             w_out[layer],
             mlp_gain[layer][None],
-            gate_all[layer],
-            up_all[layer],
-            down_all[layer],
+            gate_all,
+            up_all,
+            down_all,
         )
         stored.append((stream, queries, normed, window, middle, normed_m, gate, up, hidden, mixed, lse))
         stream = x_out
@@ -847,7 +895,7 @@
     parts = []
     for layer in reversed(range(layers)):
         x_in, queries, normed, window, middle, normed_m, gate, up, hidden, mixed, lse = stored[layer]
-        hidden_rows = gate_all.shape[1]
+        hidden_rows = gate_all.shape[0] * gate_all.shape[2]
         gy, ggate, gup, gmid, go, gain_m = call(
             mlp_back_kernel,
             (
@@ -858,15 +906,17 @@
                 shape((own, width), bf16),
                 shape((1, width), f32),
             ),
+            (),
+            [whole_spec()] * 5 + [ffn_spec(gate_all, layer)] * 3,
         )(
             upstream,
             middle,
             gate,
             up,
             mlp_gain[layer][None],
-            gate_all[layer],
-            up_all[layer],
-            down_all[layer],
+            gate_all,
+            up_all,
+            down_all,
         )
         heads = jnp.transpose(
             mixed.reshape(H, own, TILE)[:, :, HD:].astype(bf16), (1, 0, 2)
@@ -902,7 +952,9 @@
                 shape((own, width), f32),
                 shape((1, width), f32),
             ),
-        )(gq, gkv, cos_q, cos_kv, sin_all, w_in[layer], x_in, attn_gain[layer][None], gmid)
+            [pltpu.VMEM((tiles, width), bf16)],
+            [whole_spec()] * 5 + [attn_spec(w_attn, layer)] + [whole_spec()] * 3,
+        )(gq, gkv, cos_q, cos_kv, sin_all, w_attn, x_in, attn_gain[layer][None], gmid)
         gains.append((gain_a, gain_m))
 
         parts.append([gqkv, normed, go, heads, ggate, gup, normed_m, hidden, gy])

time: 459 us -> 423 us (0.922)
  the two profiles are of different devices: /device:TPU:0 before, /device:TPU:12 now
where the time goes in v4:
time: 423 us; the launch traced here: 415 us
  Pallas kernels  353 us (83%)
  local copies, waits for them, and re-layouts  38.7 us (9%)
  between operations  14.4 us (3%)
  other arithmetic  7.46 us (2%)
    pallas_call x1, Pallas kernels, sum_grads(): call(functools.partial(sum_kernel, (pair, across, up, deep), tuple(orders...  110 us
    pallas_call x2, Pallas kernels, body(): call(functools.partial(return_kernel, count, reach), shape((own, KV * TIL...  69.8 us
    pallas_call x2, Pallas kernels, body(): call(functools.partial(fetch_kernel, count, reach), shape((reach + 1, own...  49.1 us
    pallas_call x2, Pallas kernels, body(): call(functools.partial(attend_kernel, chunk_rows), (shape((own, width), f...  41.4 us
    pallas_call x2, Pallas kernels, body(): call(functools.partial(attend_back_kernel, chunk_rows), (shape((KV, GROUP...  38.8 us
    pallas_call x2, Pallas kernels, sum_grads(): call(functools.partial(weight_kernel, tuple(slots), pair), (jax.ShapeDtyp...  14.1 us
    pallas_call x2, Pallas kernels, body(): call(mlp_back_kernel, (shape((own, width), bf16), shape((own, hidden_rows...  13.4 us
    pallas_call x2, Pallas kernels, body(): call(project_back_kernel, (shape((own, tiles), bf16), shape((own, width),...  8.61 us
  transfers between devices with their start and end apart: 3, of which 0 were waited for; matrix products, arithmetic and copies ran while one was open for 6% of the time, Pallas kernels for 6%

profile of v4, /device:TPU:12, one launch (start us, length us, event | category | flops | bytes accessed | tf_op | source)
XLA Modules:
  0.0 415.5 jit_solution(4299768094268518635)
XLA Ops:
  9.9 3.9 copy.48.w_ref
  13.8 1.8 slice.45
  15.8 1.8 convert_element_type.14.x_ref
  19.8 4.0 shard_map.152
  23.8 21.3 %shard_map.153 = bf16[12,192,384]{2,1,0:T(8,128)(2,1)} custom-call(bf16[192,384]{1,0:T(8,128)(2,1)} %get-tuple-element.62.own_ref), custom_call_target="tpu_custom_call" | custom-call | tf_op jit(solution)/shard_map/pallas_call | solution.py:852
  46.4 2.0 fusion.1
  49.1 6.2 %copy.49 = bf16[4,768,576]{2,1,0:T(8,128)(2,1)} copy(bf16[4,768,576]{1,2,0:T(8,128)(2,1)} %all-gather.7.cloned.1.call-done) | data formatting | bytes 7077888 | tf_op jit(solution)/shard_map/all_gather | solution.py:831
  55.3 5.9 %copy.50 = bf16[4,768,576]{2,1,0:T(8,128)(2,1)} copy(bf16[4,768,576]{1,2,0:T(8,128)(2,1)} %all-gather.9.cloned.1.call-done) | data formatting | bytes 7077888 | tf_op jit(solution)/shard_map/all_gather | solution.py:832
  61.2 5.9 %copy.51 = bf16[4,768,576]{2,1,0:T(8,128)(2,1)} copy(bf16[4,768,576]{1,2,0:T(8,128)(2,1)} %all-gather.11.cloned.1.call-done) | data formatting | bytes 7077888 | tf_op jit(solution)/shard_map/all_gather | solution.py:833
  67.1 20.7 %shard_map.154 = (f32[192,576]{1,0:T(8,128)}, f32[192,576]{1,0:T(8,128)}, bf16[192,576]{1,0:T(8,128)(2,1)}, f32[192,1536]{1,0:T(8,128)}, f32[192,1536]{1,0:T(8,1...) custom-call(bf16[3,576,128]{2,1,0:T(8,128)(2,1)} %get-tuple-element.61.q_ref, ...), custom_call_target="tpu_custom_call" | custom-call | tf_op jit(solution)/shard_map/pallas_call | solution.py:860
  87.8 3.7 shard_map.155
  91.5 27.8 %shard_map.156 = bf16[12,192,384]{2,1,0:T(8,128)(2,1)} custom-call(bf16[192,384]{1,0:T(8,128)(2,1)} %get-tuple-element.65.own_ref), custom_call_target="tpu_custom_call" | custom-call | tf_op jit(solution)/shard_map/pallas_call | solution.py:852
  119.3 20.7 %shard_map.157 = (f32[192,576]{1,0:T(8,128)}, f32[192,576]{1,0:T(8,128)}, bf16[192,576]{1,0:T(8,128)(2,1)}, f32[192,1536]{1,0:T(8,128)}, f32[192,1536]{1,0:T(8,1...) custom-call(bf16[3,576,128]{2,1,0:T(8,128)(2,1)} %get-tuple-element.64.q_ref, ...), custom_call_target="tpu_custom_call" | custom-call | tf_op jit(solution)/shard_map/pallas_call | solution.py:860
  140.0 1.2 convert.9
  141.2 6.7 %shard_map.158 = (bf16[192,576]{1,0:T(8,128)(2,1)}, bf16[192,1536]{1,0:T(8,128)(2,1)}, bf16[192,1536]{1,0:T(8,128)(2,1)}, f32[192,576]{1,0:T(8,128)}, bf16[192,576]{1,0:T(8,128)(2,1)}, /*index=5*/f32[1,576]{1,0:T(1,128)}) custom-call(bf16[192,576]{1,0:T(8,128)(2,1)} %gx_ref.1, f32[192,576]{1,0:T(8,128)} %get-tuple-element.67.mid_ref, ...), custom_call_target="tpu_custom_call" | custom-call | tf_op jit(solution)/shard_map/pallas_call | solution.py:899
  147.9 19.4 %shard_map.159 = (f32[3,576,128]{2,1,0:T(8,128)}, bf16[2304,384]{1,0:T(8,128)(2,1)}) custom-call(bf16[192,576]{1,0:T(8,128)(2,1)} %get-tuple-element.70.go_ref, bf16[9,128,576]{2,1,0:T(8,128)(2,1)} %get-tuple-element.114.wo_ref, bf16[3,576,128]{2,1,0:T(8,128)(2,1)} %get-tuple-element.64.q_ref, bf16[2304,384]{1,0:T(8,128)(2,1)} %bitcast.56, ...), custom_call_target="tpu_custom_call" | custom-call | tf_op jit(solution)/shard_map/pallas_call | solution.py:924
  167.3 39.2 %shard_map.160.gkv_ref = f32[192,384]{1,0:T(8,128)} custom-call(bf16[12,192,384]{2,1,0:T(8,128)(2,1)} %bitcast.59), custom_call_target="tpu_custom_call" | custom-call | tf_op jit(solution)/shard_map/pallas_call | solution.py:936
  206.6 4.3 %shard_map.161 = (bf16[192,1536]{1,0:T(8,128)(2,1)}, f32[192,576]{1,0:T(8,128)}, f32[1,576]{1,0:T(1,128)}) custom-call(f32[3,576,128]{2,1,0:T(8,128)} %get-tuple-element.73.gq_ref, f32[192,384]{1,0:T(8,128)} %shard_map.160.gkv_ref, f32[192,128]{1,0:T(8,128)} %get-tuple-element.125.cq_ref, f32[192,128]{1,0:T(8,128)} %get-tuple-element.124.ckv_ref, ...), custom_call_target="tpu_custom_call" | custom-call | tf_op jit(solution)/shard_map/pallas_call | solution.py:948
  210.9 6.7 %shard_map.162 = (bf16[192,576]{1,0:T(8,128)(2,1)}, bf16[192,1536]{1,0:T(8,128)(2,1)}, bf16[192,1536]{1,0:T(8,128)(2,1)}, f32[192,576]{1,0:T(8,128)}, bf16[192,576]{1,0:T(8,128)(2,1)}, /*index=5*/f32[1,576]{1,0:T(1,128)}) custom-call(f32[192,576]{1,0:T(8,128)} %get-tuple-element.76.gx_ref, f32[192,576]{1,0:T(8,128)} %get-tuple-element.77.mid_ref, ...), custom_call_target="tpu_custom_call" | custom-call | tf_op jit(solution)/shard_map/pallas_call | solution.py:899
  217.6 19.4 %shard_map.163 = (f32[3,576,128]{2,1,0:T(8,128)}, bf16[2304,384]{1,0:T(8,128)(2,1)}) custom-call(bf16[192,576]{1,0:T(8,128)(2,1)} %get-tuple-element.80.go_ref, bf16[9,128,576]{2,1,0:T(8,128)(2,1)} %get-tuple-element.115.wo_ref, bf16[3,576,128]{2,1,0:T(8,128)(2,1)} %get-tuple-element.61.q_ref, bf16[2304,384]{1,0:T(8,128)(2,1)} %bitcast.54, ...), custom_call_target="tpu_custom_call" | custom-call | tf_op jit(solution)/shard_map/pallas_call | solution.py:924
  237.0 30.5 %shard_map.164.gkv_ref = f32[192,384]{1,0:T(8,128)} custom-call(bf16[12,192,384]{2,1,0:T(8,128)(2,1)} %bitcast.58), custom_call_target="tpu_custom_call" | custom-call | tf_op jit(solution)/shard_map/pallas_call | solution.py:936
  268.0 0.9 copy.58.o_ref
  269.3 0.8 copy.56.o_ref
  270.1 4.3 %shard_map.165 = (bf16[192,1536]{1,0:T(8,128)(2,1)}, f32[192,576]{1,0:T(8,128)}, f32[1,576]{1,0:T(1,128)}) custom-call(f32[3,576,128]{2,1,0:T(8,128)} %get-tuple-element.83.gq_ref, f32[192,384]{1,0:T(8,128)} %shard_map.164.gkv_ref, f32[192,128]{1,0:T(8,128)} %get-tuple-element.125.cq_ref, f32[192,128]{1,0:T(8,128)} %get-tuple-element.124.ckv_ref, ...), custom_call_target="tpu_custom_call" | custom-call | tf_op jit(solution)/shard_map/pallas_call | solution.py:948
  274.5 1.3 concatenate.15.refs_4_
  275.8 7.0 %shard_map.167 = (bf16[32,96,576]{2,1,0:T(8,128)(2,1)}, bf16[32,96,576]{2,1,0:T(8,128)(2,1)}) custom-call(bf16[192,1536]{1,0:T(8,128)(2,1)} %get-tuple-element.95.gqkv_ref, bf16[192,576]{1,0:T(8,128)(2,1)} %get-tuple-element.96.a_ref, bf16[192,576]{1,0:T(8,128)(2,1)} %get-tuple-element.70.go_ref, bf16[192,576]{1,0:T(8,128)(2,1)} %copy.58.o_ref, ...), custom_call_target="tpu_custom_call" | custom-call | tf_op jit(solution)/shard_map/pallas_call | solution.py:735
  282.8 7.0 %shard_map.166 = (bf16[32,96,576]{2,1,0:T(8,128)(2,1)}, bf16[32,96,576]{2,1,0:T(8,128)(2,1)}) custom-call(bf16[192,1536]{1,0:T(8,128)(2,1)} %get-tuple-element.87.gqkv_ref, bf16[192,576]{1,0:T(8,128)(2,1)} %get-tuple-element.88.a_ref, bf16[192,576]{1,0:T(8,128)(2,1)} %get-tuple-element.80.go_ref, bf16[192,576]{1,0:T(8,128)(2,1)} %copy.56.o_ref, ...), custom_call_target="tpu_custom_call" | custom-call | tf_op jit(solution)/shard_map/pallas_call | solution.py:735
  289.8 110.0 %shard_map.168 = (f32[96,576]{1,0:T(8,128)}, f32[96,576]{1,0:T(8,128)}, f32[96,576]{1,0:T(8,128)}, f32[96,576]{1,0:T(8,128)}, f32[8,576]{1,0:T(8,128)}) custom-call(bf16[32,96,576]{2,1,0:T(8,128)(2,1)} %get-tuple-element.94.refs_0_, bf16[32,96,576]{2,1,0:T(8,128)(2,1)} %get-tuple-element.102.refs_1_, bf16[32,96,576]{2,1,0:T(8,128)(2,1)} %get-tuple-element.103.refs_2_, ...), custom_call_target="tpu_custom_call" | custom-call | tf_op jit(solution)/shard_map/pallas_call | solution.py:781
  401.7 1.0 slice_bitcast_fusion.1
  402.7 1.0 slice_bitcast_fusion
  403.7 1.0 slice_bitcast_fusion.5
  404.7 1.0 slice_bitcast_fusion.4
  (58 shorter events, 12.6 us)
Async XLA Ops:
  7.2 41.9 %all-gather.7.cloned.1.call-start = ((), (), s32[]{:S(2)}) async-start(), calls=%async_computation | async-start | bytes 5308416 | tf_op jit(solution)/shard_map/all_gather | solution.py:831
  7.9 2.0 copy-start
  7.9 47.4 %all-gather.9.cloned.1.call-start = ((), (), s32[]{:S(2)}) async-start(), calls=%async_computation.1 | async-start | bytes 5308416 | tf_op jit(solution)/shard_map/all_gather | solution.py:832
  8.7 52.5 %all-gather.11.cloned.1.call-start = ((), (), s32[]{:S(2)}) async-start(), calls=%async_computation.2 | async-start | bytes 5308416 | tf_op jit(solution)/shard_map/all_gather | solution.py:833
  13.8 3.8 copy-start.8
  13.8 4.1 copy-start.3
  23.8 22.6 %copy-start.1 = (bf16[2,576,576]{1,2,0:T(8,128)(2,1)S(1)}, bf16[2,576,576]{1,2,0:T(8,128)(2,1)}, u32[]{:S(2)}) copy-start(bf16[2,576,576]{1,2,0:T(8,128)(2,1)} %slice.45) | copy-start | bytes 3981316
  46.4 2.0 copy-start.4
  167.3 39.3 %copy-start.2 = (f32[3,576,128]{2,1,0:T(8,128)S(1)}, f32[3,576,128]{2,1,0:T(8,128)}, u32[]{:S(2)}) copy-start(f32[3,576,128]{2,1,0:T(8,128)} %get-tuple-element.81.o_ref) | copy-start | bytes 2654212
  270.1 4.3 %copy-start.5 = (f32[1,576]{1,0:T(1,128)S(1)}, f32[1,576]{1,0:T(1,128)}, u32[]{:S(2)}) copy-start(f32[1,576]{1,0:T(1,128)} %get-tuple-element.108) | copy-start | bytes 6916
  270.1 4.3 %copy-start.6 = (f32[1,576]{1,0:T(1,128)S(1)}, f32[1,576]{1,0:T(1,128)}, u32[]{:S(2)}) copy-start(f32[1,576]{1,0:T(1,128)} %get-tuple-element.107) | copy-start | bytes 6916
  270.1 4.3 %copy-start.7 = (f32[1,576]{1,0:T(1,128)S(1)}, f32[1,576]{1,0:T(1,128)}, u32[]{:S(2)}) copy-start(f32[1,576]{1,0:T(1,128)} %get-tuple-element.106) | copy-start | bytes 6916
Sparse Core Ops, SparseCore 0:
  9.5 14.0 all-gather.6
  25.2 13.8 all-gather.8
  40.7 14.0 all-gather.10
